TPU v7x, 128 devices: a whole 4x4x4 slice. The times are simulated.
128 devices in a mesh: section: 8 (over y_lo, x), peer: 16 (over y_hi, z, core).
Axes of the slice: x: 4, y: 4 (y_hi: 2, y_lo: 2; y = y_hi * 2 + y_lo), z: 4, core: 2. Of those that a mesh axis runs over, the one named last changes fastest.
Arguments:
- queries: bfloat16 [256, 16384], P(('section', 'peer')), may hold values from -256 to 256
- residual: bfloat16 [256, 16384], P(('section', 'peer')), may hold values from -3 to 3
- key_tile_store: bfloat16 [8, 256, 256, 1024], P('section', 'peer'), may hold values from -6 to 6
- value_tile_store: bfloat16 [8, 256, 256, 1024], P('section', 'peer'), may hold values from -6 to 6
- lengths: int32 [8, 32], P('section'), may hold values from 2 to 16384, as said below
- tile_request: int32 [8, 256], P('section', 'peer'), may hold values from 0 to 31, as said below
- tile_position: int32 [8, 256], P('section', 'peer'), may hold values from 0 to 63, as said below
Outputs:
- attended: bfloat16 [256, 16384], P(('section', 'peer'))
- next_hidden: bfloat16 [256, 16384], P(('section', 'peer'))
Inputs may be any that keep to these rules, and one draw needn't show every extreme that they name: `tile_request`: every slot of a section is owned; each request of a section owns between 1 and 64 slots and exactly one request of each section owns 64; a request's slots lie in a run of consecutive slots, wrapping around the section's end. `tile_position`: the slots of a request hold its tile indices 0 to its slot count minus one, once each. `lengths`: A request owning c slots has a length above (c - 1) * 256 and at most c * 256; the request of each section that owns 64 slots has length 16384.
All inputs are finite; a program needn't handle non-finite values.
Results may differ from a plain program's by a relative error of at most 0.025.
Values may be sent and summed in bfloat16 or wider, within the bound.
A program may use at most 128 MiB of HBM per device.

v0:
```python
import jax
import jax.numpy as jnp
from jax import lax
from jax.sharding import PartitionSpec as P

QUERY_HEADS = 128
KEY_VALUE_HEADS = 8
HEAD_SIZE = 128
TILE_TOKENS = 256


def from_behind(block, axis, distance):
    devices = range(lax.axis_size(axis))
    route = [((i - distance) % len(devices), i) for i in devices]
    return lax.ppermute(block, axis, route)


def local(
    queries, residual, key_tile_store, value_tile_store, lengths, tile_request, tile_position
):
    requests_here = queries.shape[0]
    query_group_width = QUERY_HEADS // KEY_VALUE_HEADS
    collected_rows = lax.all_gather(queries, "peer", axis=0, tiled=True)
    section_rows = collected_rows.shape[0]
    count_of_slots = key_tile_store.shape[1]
    owning_requests = tile_request[0]
    places = tile_position[0]
    section_lengths = lengths[0]
    key_row_block = key_tile_store[0].reshape(
        count_of_slots, TILE_TOKENS, KEY_VALUE_HEADS, HEAD_SIZE
    )
    value_row_block = value_tile_store[0].reshape(
        count_of_slots, TILE_TOKENS, KEY_VALUE_HEADS, HEAD_SIZE
    )
    selected_slots = jnp.take(collected_rows, owning_requests, axis=0).reshape(
        count_of_slots, KEY_VALUE_HEADS, query_group_width, HEAD_SIZE
    )
    scores = jnp.einsum(
        "tgjd,tpgd->tgjp", selected_slots, key_row_block, preferred_element_type=jnp.float32
    ) * HEAD_SIZE ** (-0.5)
    offsets = places[:, None] * TILE_TOKENS + jnp.arange(TILE_TOKENS, dtype=jnp.int32)[None, :]
    limits = jnp.take(section_lengths, owning_requests, axis=0)
    usable = offsets < limits[:, None]
    scores = jnp.where(usable[:, None, None, :], scores, -jnp.inf)
    tile_peak = jnp.max(scores, axis=3)
    member = owning_requests[None, :] == jnp.arange(section_rows, dtype=jnp.int32)[:, None]
    member_wide = member.astype(jnp.float32)
    local_peak = jnp.max(jnp.where(member[:, :, None, None], tile_peak[None], -1e30), axis=1)
    global_peak = lax.pmax(local_peak, "peer")
    weights = jnp.exp(scores - jnp.take(global_peak, owning_requests, axis=0)[..., None]).astype(
        jnp.bfloat16
    )
    totals = jnp.sum(weights.astype(jnp.float32), axis=3)
    mixture = jnp.einsum(
        "tgjp,tpgd->tgjd", weights, value_row_block, preferred_element_type=jnp.float32
    )
    request_total = jnp.einsum("rt,tgj->rgj", member_wide, totals, precision=lax.Precision.HIGHEST)
    request_mix = jnp.einsum("rt,tgjd->rgjd", member_wide, mixture, precision=lax.Precision.HIGHEST)
    mix_local = request_mix.reshape(section_rows, QUERY_HEADS * HEAD_SIZE)
    total_local = request_total.reshape(section_rows, QUERY_HEADS)
    mix_home, total_home = (
        lax.psum_scatter(
            mix_local.astype(jnp.bfloat16), "peer", scatter_dimension=0, tiled=True
        ).astype(jnp.float32),
        lax.psum_scatter(
            total_local.astype(jnp.bfloat16), "peer", scatter_dimension=0, tiled=True
        ).astype(jnp.float32),
    )
    attended = (
        mix_home.reshape(requests_here, QUERY_HEADS, HEAD_SIZE) / total_home[..., None]
    ).reshape(requests_here, QUERY_HEADS * HEAD_SIZE)
    attended = attended.astype(jnp.bfloat16)
    held_rows = lax.optimization_barrier(attended)
    handed = (residual.astype(jnp.float32) + held_rows.astype(jnp.float32)).astype(jnp.bfloat16)
    next_hidden = from_behind(handed, "section", 1)
    return (attended, next_hidden)


def solution(mesh):
    in_specs = (
        P(("section", "peer"), None),
        P(("section", "peer"), None),
        P("section", "peer", None, None),
        P("section", "peer", None, None),
        P("section", None),
        P("section", "peer"),
        P("section", "peer"),
    )
    out_specs = (P(("section", "peer"), None), P(("section", "peer"), None))
    return jax.shard_map(local, mesh=mesh, in_specs=in_specs, out_specs=out_specs, check_vma=False)
```

profile of v0, /device:TPU:0, one launch (start us, length us, event | category | flops | bytes accessed | tf_op | source)
XLA Modules:
  0.0 298.6 jit_solution(15267893365153376614)
XLA Ops:
  7.2 0.7 all-gather.3.cloned.1.call-update
  8.0 8.8 %copy.31 = bf16[512,8,8,128]{3,2,1,0:T(8,128)(2,1)} copy(bf16[512,8,8,128]{3,1,2,0:T(8,128)(2,1)} %bitcast.47) | data formatting | bytes 16777216
  16.7 8.8 %copy.32 = bf16[512,8,8,128]{3,2,1,0:T(8,128)(2,1)} copy(bf16[512,8,8,128]{3,1,2,0:T(8,128)(2,1)} %bitcast.48) | data formatting | bytes 16777216
  25.5 0.7 gather_fusion
  26.4 31.6 %all-gather.3.cloned.1.call-done = bf16[16,2,16384]{2,1,0:T(2,128)(2,1)} async-done(((bf16[1,2,16384]{2,1,0:T(2,128)(2,1)}), bf16[16,2,16384]{2,1,0:T(2,128)(2,1)}) %all-gather.3.cloned.1.call-update) | async-done | bytes 1048592 | tf_op jit(solution)/shard_map/all_gather | solution.py:23
  57.9 1.5 reshape.152
  59.4 0.9 gather_fusion.1
  60.4 5.8 %fusion.4 = (f32[16,8,16]{2,1,0:T(8,128)S(1)}, f32[16,8,16,256]{3,2,1,0:T(8,128)S(1)}) fusion(pred[16,256]{1,0:T(8,128)(4,1)S(1)} %add_compare_fusion, bf16[16,256,8,128]{3,2,1,0:T(8,128)(2,1)} %bitcast.46, bf16[16,8,16,128]{3,2,1,0:T(8,128)(2,1)S(1)} %bitcast.53, pred[16]{0:T(512)(128)(4,1)S(1)} %get-tuple-element.3), kind=kOutput, calls=%fused_computation.10 | convolution fusion | flops 136050688 | bytes 11022352 | tf_op jit(solution)/shard_map/tgjd,tpgd->tgjp/dot_general | solution.py:38
  66.2 0.3 select_reduce_fusion
  66.6 68.0 %pmax.7 = f32[32,8,16]{2,1,0:T(8,128)S(1)} all-reduce(f32[32,8,16]{2,1,0:T(8,128)S(1)} %copy.25), channel_id=1, replica_groups=mesh['section'=8,'peer'=16] {'peer'}, use_global_device_ids=true, to_apply=%region_2.3 | all-reduce | flops 4096 | bytes 32768 | tf_op jit(solution)/shard_map/pmax | solution.py:49
  134.7 0.6 gather_fusion.2
  135.3 4.7 %fusion = f32[16,8,16,128]{3,2,1,0:T(8,128)S(1)} fusion(bf16[16,256,8,128]{3,2,1,0:T(8,128)(2,1)} %bitcast.49, f32[16,8,16,256]{3,2,1,0:T(8,128)S(1)} %get-tuple-element.5, f32[16,8,16]{2,1,0:T(8,128)S(1)} %broadcast_select_fusion, pred[16,256]{1,0:T(8,128)(4,1)S(1)} %add_compare_fusion), kind=kOutput, calls=%fused_computation.3 | convolution fusion | flops 136314880 | bytes 11546624 | tf_op jit(solution)/shard_map/tgjp,tpgd->tgjd/dot_general | solution.py:54
  140.1 1.6 convolution_convert_fusion
  141.6 0.4 copy.28
  142.1 1.7 copy.47
  143.8 0.6 dynamic-slice
  145.1 0.9 convert_reduce_fusion
  146.1 0.3 convolution_convert_fusion.1
  146.4 33.7 %all-reduce.1 = bf16[32,128]{1,0:T(8,128)(2,1)S(1)} all-reduce(bf16[32,128]{1,0:T(8,128)(2,1)S(1)} %convolution_convert_fusion.1), channel_id=3, replica_groups=mesh['section'=8,'peer'=16] {'peer'}, use_global_device_ids=true, to_apply=%region_5.6.clone | all-reduce | flops 4096 | bytes 16384
  180.2 103.3 %all-reduce.4.cloned.1.call-done = bf16[32,16384]{1,0:T(8,128)(2,1)} async-done(((bf16[32,16384]{1,0:T(8,128)(2,1)}), bf16[32,16384]{1,0:T(8,128)(2,1)}) %all-reduce.4.cloned.1.call-update) | async-done | bytes 1048592
  283.5 1.1 fusion.9
  284.7 1.5 collective-permute-start
  286.2 4.9 %collective-permute-done = bf16[2,16384]{1,0:T(2,128)(2,1)S(1)} collective-permute-done((bf16[2,16384]{1,0:T(2,128)(2,1)S(1)}, bf16[2,16384]{1,0:T(2,128)(2,1)S(1)}, u32[]{:S(2)}, u32[]{:S(2)}) %collective-permute-start) | collective-permute-done | bytes 65568 | tf_op jit(solution)/shard_map/ppermute | solution.py:15
  291.1 0.6 copy.50
  (28 shorter events, 0.8 us)
Async XLA Ops:
  7.2 18.4 %copy-start = (s32[1,32]{1,0:T(1,128)S(1)}, s32[1,32]{1,0:T(1,128)}, u32[]{:S(2)}) copy-start(s32[1,32]{1,0:T(1,128)} %param.11) | copy-start | bytes 388
  7.2 50.8 %all-gather.3.cloned.1.call-start = ((), (), s32[]{:S(2)}) async-start(), calls=%async_computation | async-start | bytes 1114112 | tf_op jit(solution)/shard_map/all_gather | solution.py:23
  7.9 275.6 %all-reduce.4.cloned.1.call-start = ((), (), s32[]{:S(2)}) async-start(), calls=%async_computation.1 | async-start | bytes 2097152
  16.7 8.8 %copy-start.3 = (s32[1,16]{1,0:T(1,128)S(1)}, s32[1,16]{1,0:T(1,128)}, u32[]{:S(2)}) copy-start(s32[1,16]{1,0:T(1,128)} %param.12) | copy-start | bytes 196
  16.7 9.5 %copy-start.4 = (s32[1,16]{1,0:T(1,128)S(1)}, s32[1,16]{1,0:T(1,128)}, u32[]{:S(2)}) copy-start(s32[1,16]{1,0:T(1,128)} %param.13) | copy-start | bytes 196
  142.1 1.8 copy-start.5
  143.8 140.8 %copy-start.2 = (bf16[2,16384]{1,0:T(2,128)(2,1)S(1)}, bf16[2,16384]{1,0:T(2,128)(2,1)}, u32[]{:S(2)}) copy-start(bf16[2,16384]{1,0:T(2,128)(2,1)} %param.8) | copy-start | bytes 196612
  284.6 7.2 %copy-start.1 = (bf16[2,16384]{1,0:T(2,128)(2,1)}, bf16[2,16384]{1,0:T(2,128)(2,1)S(1)}, u32[]{:S(2)}) copy-start(bf16[2,16384]{1,0:T(2,128)(2,1)S(1)} %fusion.9) | copy-start | bytes 196612
  284.7 6.4 %collective-permute-start = (bf16[2,16384]{1,0:T(2,128)(2,1)S(1)}, bf16[2,16384]{1,0:T(2,128)(2,1)S(1)}, u32[]{:S(2)}, u32[]{:S(2)}) collective-permute-start(bf16[2,16384]{1,0:T(2,128)(2,1)S(1)} %add_convert_fusion), channel_id=1, source_target_pairs={{112,0},{0,16},{16,32},{32,48},{48,64},{64,80},{80,96},{96,112},{1... | collective-permute-start | bytes 196616 | tf_op jit(solution)/shard_map/ppermute | solution.py:15
Sparse Core Ops, SparseCore 0:
  10.5 47.4 all-gather.2
  143.9 139.5 all-reduce.3
where the time goes:
time: 299 us
  waiting for transfers between devices  140 us (47%)
  blocking collectives  102 us (34%)
  local copies, waits for them, and re-layouts  24.8 us (8%)
  between operations  14.9 us (5%)
  matrix products  12.3 us (4%)
    unnamed x3, waiting for transfers between devices  104 us
    pmax x1, blocking collectives, local(): global_peak = lax.pmax(local_peak, 'peer')  68 us
    unnamed x1, blocking collectives  33.7 us
    all_gather x1, waiting for transfers between devices, local(): collected_rows = lax.all_gather(queries, 'peer', axis=0, tiled=True)  31.6 us
    unnamed x20, local copies, waits for them, and re-layouts  22.1 us
  transfers between devices with their start and end apart: 3, of which 3 were waited for; matrix products, arithmetic and copies ran while one was open for 7% of the time, Pallas kernels for 0%

commit v1 on v0

v1 whole, which is shorter than its diff:
```python
import functools

import jax
import jax.numpy as jnp
from jax import lax
from jax.experimental import pallas as pl
from jax.experimental.pallas import tpu as pltpu
from jax.sharding import PartitionSpec as P

PEERS = 16
SECTIONS = 8
SLOTS = 16
TILE = 256
HEADS = 128
HEAD = 128
REQUESTS = 32
PHASES = 4
PHASE_HEADS = HEADS // PHASES
GROUP = 16
UNROLL = 4
SCALE = HEAD ** (-0.5)
MESH = pl.DeviceIdType.MESH


def kernel(
    q_hbm, res_hbm, k_hbm, v_hbm, len_ref, req_ref, pos_ref,
    att_ref, nxt_ref, prev_res_ref,
    q_in, q_f32, q_send, gq0, gq1, gq2, gq3, kbuf, vbuf,
    x_f32, x_send, xr0, xr1, xr2, xr3,
    meta_f32, meta_send, mr0, mr1, mr2, mr3,
    fin_f32, fin_send,
    q_sem, kv_sem, gq_send_sem, gq_recv_sem, x_send_sem, x_recv_sem,
    m_send_sem, m_recv_sem, fin_send_sem, att_recv_sem, nxt_recv_sem, res_send_sem, res_recv_sem,
):
    gq = (gq0, gq1, gq2, gq3)
    xr = (xr0, xr1, xr2, xr3)
    mr = (mr0, mr1, mr2, mr3)
    me = lax.axis_index("peer")
    section = lax.axis_index("section")
    after = lax.rem(section + 1, SECTIONS)
    before = lax.rem(section + SECTIONS - 1, SECTIONS)

    q_copy = pltpu.make_async_copy(q_hbm, q_in, q_sem)
    q_copy.start()
    loads = []
    for p in range(PHASES):
        cols = pl.ds(p * 256, 256)
        for i, (src, dst) in enumerate(((k_hbm, kbuf), (v_hbm, vbuf))):
            load = pltpu.make_async_copy(
                src.at[0, :, :, cols], dst.at[p], kv_sem.at[p, i])
            load.start()
            loads.append(load)

    barrier = pltpu.get_barrier_semaphore()

    def greet_peer(d, carry):
        pl.semaphore_signal(
            barrier, inc=1, device_id=(section, lax.rem(me + d, PEERS)), device_id_type=MESH)
        return carry

    lax.fori_loop(1, PEERS, greet_peer, 0)

    def greet_before(d, carry):
        pl.semaphore_signal(
            barrier, inc=1, device_id=(before, d), device_id_type=MESH)
        return carry

    lax.fori_loop(0, PEERS, greet_before, 0)

    q_copy.wait()
    for h in range(HEADS):
        piece = q_in[:, h * HEAD:(h + 1) * HEAD].astype(jnp.float32)
        q_f32[0, h:h + 1, :] = piece[0:1]
        q_f32[1, h:h + 1, :] = piece[1:2]
    for p in range(PHASES):
        q_send[p] = q_f32[:, p * PHASE_HEADS:(p + 1) * PHASE_HEADS, :].astype(jnp.bfloat16)

    pl.semaphore_wait(barrier, 2 * PEERS - 1)

    for p in range(PHASES):
        def send_q(d, carry, p=p):
            pltpu.make_async_remote_copy(
                src_ref=q_send.at[p], dst_ref=gq[p].at[pl.ds(2 * me, 2)],
                send_sem=gq_send_sem, recv_sem=gq_recv_sem.at[p],
                device_id=(section, lax.rem(me + d, PEERS)), device_id_type=MESH).start()
            return carry

        pltpu.make_async_copy(
            q_send.at[p], gq[p].at[pl.ds(2 * me, 2)], gq_recv_sem.at[p]).start()
        lax.fori_loop(1, PEERS, send_q, 0)
    pass_residual = pltpu.make_async_remote_copy(
        src_ref=res_hbm, dst_ref=prev_res_ref, send_sem=res_send_sem, recv_sem=res_recv_sem,
        device_id=(after, me), device_id_type=MESH)
    pass_residual.start()

    token = lax.broadcasted_iota(jnp.int32, (PHASE_HEADS, TILE), 1)
    lane = lax.broadcasted_iota(jnp.int32, (PHASE_HEADS, 128), 1)
    zero_block = jnp.zeros((GROUP, HEAD), jnp.bfloat16)

    def merge(p):
        for ref, recv in ((xr[p], x_recv_sem.at[p]), (mr[p], m_recv_sem.at[p])):
            pltpu.make_async_copy(ref, ref, recv).wait()
        rows = jnp.concatenate([mr[p][e] for e in range(PEERS)], axis=0)
        lanes = lax.broadcasted_iota(jnp.int32, (8, 128), 1)
        own = lax.broadcasted_iota(jnp.int32, (8, 128), 0)
        mine = lanes // 16 == own

        def line(at):
            parts = []
            for half in (rows[0:8], rows[8:16]):
                if at:
                    half = pltpu.roll(half, 128 - at, 1)
                turned = pltpu.roll(half, 0, 1, stride=16, stride_axis=0)
                parts.append(jnp.sum(jnp.where(mine, turned, 0.0), axis=0, keepdims=True))
            return jnp.concatenate(parts, axis=1)

        order = lax.broadcasted_iota(jnp.int32, (REQUESTS, 2 * 128), 0)
        request = (2 * lax.rem(order, 16) + order // 16).astype(jnp.float32)
        for b in range(2):
            peak, total, code = line(64 * b), line(64 * b + 16), line(64 * b + 32)
            member = code == request
            held = jnp.where(member, peak, -jnp.inf)
            top = jnp.max(held, axis=1, keepdims=True)
            weight = jnp.exp(held - top).astype(jnp.bfloat16)
            whole = jnp.sum(weight.astype(jnp.float32) * total, axis=1, keepdims=True)
            mixed = jnp.dot(weight, xr[p][b], preferred_element_type=jnp.float32) / whole
            for i in range(2):
                fin_f32[pl.ds(2 * (2 * p + b) + i, 16, stride=16), :] = mixed[16 * i:16 * i + 16]

    for p in range(PHASES):
        pltpu.make_async_copy(gq[p], gq[p], gq_recv_sem.at[p]).wait()
        loads[2 * p].wait()
        loads[2 * p + 1].wait()

        def tiles(step, carry, p=p):
            peak, total, mix, meta = carry
            for u in range(UNROLL):
                t = step * UNROLL + u
                owner = req_ref[0, t]
                same = (t > 0) & (owner == req_ref[0, jnp.maximum(t - 1, 0)])
                closing = (t == SLOTS - 1) | (owner != req_ref[0, jnp.minimum(t + 1, SLOTS - 1)])
                code = jnp.where(closing, owner, -1).astype(jnp.float32)
                limit = len_ref[0, owner] - pos_ref[0, t] * TILE
                q = gq[p][owner]
                wide = jnp.concatenate(
                    [jnp.concatenate([q[:GROUP], zero_block], axis=1),
                     jnp.concatenate([zero_block, q[GROUP:]], axis=1)], axis=0)
                score = lax.dot_general(
                    wide, kbuf[p, t], (((1,), (1,)), ((), ())),
                    preferred_element_type=jnp.float32) * SCALE
                score = jnp.where(token < limit, score, -jnp.inf)
                old = jnp.where(same, peak, -jnp.inf)
                peak = jnp.maximum(old, jnp.max(score, axis=1, keepdims=True))
                keep = jnp.exp(old - peak)
                weight = jnp.exp(score - peak).astype(jnp.bfloat16)
                total = keep * total + jnp.sum(weight.astype(jnp.float32), axis=1, keepdims=True)
                both = jnp.dot(weight, vbuf[p, t], preferred_element_type=jnp.float32)
                mix = keep * mix + jnp.concatenate(
                    [both[:GROUP, :HEAD], both[GROUP:, HEAD:]], axis=0)
                x_f32[pl.ds(t, PHASE_HEADS, stride=SLOTS), :] = mix
                meta = jnp.where(lane == t, peak, meta)
                meta = jnp.where(lane == 16 + t, total, meta)
                meta = jnp.where(lane == 32 + t, code, meta)
            return peak, total, mix, meta

        _, _, _, meta = lax.fori_loop(
            0, SLOTS // UNROLL, tiles,
            (jnp.zeros((PHASE_HEADS, 1), jnp.float32), jnp.zeros((PHASE_HEADS, 1), jnp.float32),
             jnp.zeros((PHASE_HEADS, HEAD), jnp.float32), jnp.zeros((PHASE_HEADS, 128), jnp.float32)))
        x_send[p] = x_f32[...].astype(jnp.bfloat16).reshape(PEERS, 2, SLOTS, HEAD)
        meta_f32[...] = meta
        line = meta_f32[pl.ds(0, PEERS, stride=2), :] + pltpu.roll(
            meta_f32[pl.ds(1, PEERS, stride=2), :], 64, 1)
        for j in range(PEERS):
            meta_send[p, j] = line[j:j + 1]

        def send_x(d, carry, p=p):
            to = lax.rem(me + d, PEERS)
            pltpu.make_async_remote_copy(
                src_ref=x_send.at[p, to], dst_ref=xr[p].at[:, pl.ds(SLOTS * me, SLOTS), :],
                send_sem=x_send_sem, recv_sem=x_recv_sem.at[p],
                device_id=(section, to), device_id_type=MESH).start()
            pltpu.make_async_remote_copy(
                src_ref=meta_send.at[p, to], dst_ref=mr[p].at[me],
                send_sem=m_send_sem, recv_sem=m_recv_sem.at[p],
                device_id=(section, to), device_id_type=MESH).start()
            return carry

        pltpu.make_async_copy(
            x_send.at[p, me], xr[p].at[:, pl.ds(SLOTS * me, SLOTS), :], x_recv_sem.at[p]).start()
        pltpu.make_async_copy(
            meta_send.at[p, me], mr[p].at[me], m_recv_sem.at[p]).start()
        lax.fori_loop(1, PEERS, send_x, 0)
        if p > 0:
            merge(p - 1)
    merge(PHASES - 1)

    fin_send[...] = fin_f32[...].astype(jnp.bfloat16).reshape(PEERS, 16, HEAD)

    def send_home(d, carry):
        to = lax.rem(me + d, PEERS)
        pltpu.make_async_remote_copy(
            src_ref=fin_send.at[to], dst_ref=att_ref.at[me],
            send_sem=fin_send_sem, recv_sem=att_recv_sem,
            device_id=(section, to), device_id_type=MESH).start()
        return carry

    def send_after(d, carry):
        to = lax.rem(me + d, PEERS)
        pltpu.make_async_remote_copy(
            src_ref=fin_send.at[to], dst_ref=nxt_ref.at[me],
            send_sem=fin_send_sem, recv_sem=nxt_recv_sem,
            device_id=(after, to), device_id_type=MESH).start()
        return carry

    lax.fori_loop(0, PEERS, send_after, 0)
    pltpu.make_async_copy(fin_send.at[me], att_ref.at[me], att_recv_sem).start()
    lax.fori_loop(1, PEERS, send_home, 0)

    for p in range(PHASES):
        pltpu.make_async_copy(
            gq[p].at[pl.ds(0, 30)], gq[p].at[pl.ds(0, 30)], gq_send_sem).wait()
        pltpu.make_async_copy(
            x_send.at[p, pl.ds(0, 15)], x_send.at[p, pl.ds(0, 15)], x_send_sem).wait()
        pltpu.make_async_copy(
            meta_send.at[p, pl.ds(0, 15)], meta_send.at[p, pl.ds(0, 15)], m_send_sem).wait()
    pass_residual.wait()
    pltpu.make_async_copy(fin_send, fin_send, fin_send_sem).wait()
    pltpu.make_async_copy(
        fin_send.at[pl.ds(0, 15)], fin_send.at[pl.ds(0, 15)], fin_send_sem).wait()
    pltpu.make_async_copy(att_ref, att_ref, att_recv_sem).wait()
    pltpu.make_async_copy(nxt_ref, nxt_ref, nxt_recv_sem).wait()


def local(
    queries, residual, key_tile_store, value_tile_store, lengths, tile_request, tile_position
):
    any_spec = pl.BlockSpec(memory_space=pl.ANY)
    smem_spec = pl.BlockSpec(memory_space=pltpu.SMEM)
    vmem_spec = pl.BlockSpec(memory_space=pltpu.VMEM)
    dma = pltpu.SemaphoreType.DMA
    bf16, f32 = jnp.bfloat16, jnp.float32
    scratch = (
        [pltpu.VMEM((2, HEADS * HEAD), bf16), pltpu.VMEM((2, HEADS, HEAD), f32),
         pltpu.VMEM((PHASES, 2, PHASE_HEADS, HEAD), bf16)]
        + [pltpu.VMEM((REQUESTS, PHASE_HEADS, HEAD), bf16)] * PHASES
        + [pltpu.VMEM((PHASES, SLOTS, TILE, 256), bf16)] * 2
        + [pltpu.VMEM((PHASE_HEADS * SLOTS, HEAD), f32),
           pltpu.VMEM((PHASES, PEERS, 2, SLOTS, HEAD), bf16)]
        + [pltpu.VMEM((2, PEERS * SLOTS, HEAD), bf16)] * PHASES
        + [pltpu.VMEM((PHASE_HEADS, 128), f32), pltpu.VMEM((PHASES, PEERS, 1, 128), f32)]
        + [pltpu.VMEM((PEERS, 1, 128), f32)] * PHASES
        + [pltpu.VMEM((PEERS * 16, HEAD), f32), pltpu.VMEM((PEERS, 16, HEAD), bf16)]
        + [dma, dma((PHASES, 2)), dma, dma((PHASES,)), dma, dma((PHASES,)), dma, dma((PHASES,)),
           dma, dma, dma, dma, dma]
    )
    att, nxt, prev_res = pl.pallas_call(
        kernel,
        out_shape=(
            jax.ShapeDtypeStruct((PEERS, 16, HEAD), bf16),
            jax.ShapeDtypeStruct((PEERS, 16, HEAD), bf16),
            jax.ShapeDtypeStruct(residual.shape, bf16),
        ),
        in_specs=[any_spec] * 4 + [smem_spec] * 3,
        out_specs=[vmem_spec, vmem_spec, vmem_spec],
        scratch_shapes=scratch,
        compiler_params=pltpu.CompilerParams(
            collective_id=0, has_side_effects=True, vmem_limit_bytes=60 * 1024 * 1024),
    )(queries, residual, key_tile_store, value_tile_store, lengths, tile_request, tile_position)

    def home(block):
        block = block.reshape(PEERS, PHASES, 2, 2, HEAD)
        return block.transpose(3, 1, 0, 2, 4).reshape(2, HEADS * HEAD)

    attended = home(att)
    next_hidden = (prev_res.astype(f32) + home(nxt).astype(f32)).astype(bf16)
    return attended, next_hidden


def solution(mesh):
    in_specs = (
        P(("section", "peer"), None),
        P(("section", "peer"), None),
        P("section", "peer", None, None),
        P("section", "peer", None, None),
        P("section", None),
        P("section", "peer"),
        P("section", "peer"),
    )
    out_specs = (P(("section", "peer"), None), P(("section", "peer"), None))
    return jax.shard_map(local, mesh=mesh, in_specs=in_specs, out_specs=out_specs, check_vma=False)
```

time: 299 us -> 56.8 us (0.19)
  the two profiles are of different devices: /device:TPU:0 before, /device:TPU:1 now
where the time goes in v1:
time: 56.8 us; the launch traced here: 56.6 us
  Pallas kernels  51.8 us (91%)
  local copies, waits for them, and re-layouts  2.55 us (4%)
  other arithmetic  1.54 us (3%)
  between operations  0.66 us (1%)
    pallas_call x1, Pallas kernels, local(): pl.pallas_call(kernel, out_shape=(jax.ShapeDtypeStruct((PEERS, 16, HEAD),...  51.8 us
    convert_element_type x1, other arithmetic, local(): next_hidden = (prev_res.astype(f32) + home(nxt).astype(f32)).astype(bf16)  1.54 us

profile of v1, /device:TPU:1, one launch (start us, length us, event | category | flops | bytes accessed | tf_op | source)
XLA Modules:
  0.0 56.6 jit_solution(17373122333750887614)
XLA Ops:
  0.6 51.8 %shard_map.86 = (bf16[16,16,128]{2,1,0:T(8,128)(2,1)}, bf16[16,16,128]{2,1,0:T(8,128)(2,1)}, bf16[2,16384]{1,0:T(2,128)(2,1)}) custom-call(bf16[2,16384]{1,0:T(2,128)(2,1)} %q_hbm.1, bf16[2,16384]{1,0:T(2,128)(2,1)} %res_hbm.1, bf16[1,16,256,1024]{3,2,1,0:T(8,128)(2,1)} %k_hbm.1, bf16[1,16,256,1024]{3,2,1,0:T(8,128)(2,1)} %v_hbm.1, s32[1,32]{1,0:T(1,128)} %len_ref.1, ...), custom_call_target="tpu_custom_call" | custom-call | tf_op jit(solution)/shard_map/pallas_call | solution.py:257
  52.5 0.9 %copy.9 = bf16[2,4,16,2,128]{4,3,2,1,0:T(2,128)(2,1)S(1)} copy(bf16[2,4,16,2,128]{4,0,3,1,2:T(2,128)(2,1)} %bitcast.12) | data formatting | bytes 131072 | tf_op jit(solution)/shard_map/transpose | solution.py:273
  53.3 0.7 %reshape.17 = bf16[2,16384]{1,0:T(2,128)(2,1)} reshape(bf16[2,4,16,2,128]{4,3,2,1,0:T(2,128)(2,1)S(1)} %copy.9) | data formatting | bytes 131072 | tf_op jit(solution)/shard_map/reshape | solution.py:273
  54.0 0.9 %copy.12 = f32[16,4,2,2,128]{4,2,0,1,3:T(2,128)S(1)} copy(bf16[16,4,2,2,128]{4,3,2,1,0:T(2,128)(2,1)} %bitcast.11) | data formatting | bytes 196608 | tf_op jit(solution)/shard_map/convert_element_type | solution.py:276
  54.9 0.2 reshape.18
  55.0 1.5 %add_convert_fusion = bf16[2,16384]{1,0:T(2,128)(2,1)} fusion(f32[2,16384]{1,0:T(2,128)S(1)} %reshape.18, bf16[2,16384]{1,0:T(2,128)(2,1)} %get-tuple-element.6), kind=kLoop, calls=%fused_computation.1 | loop fusion | flops 98304 | bytes 262144 | tf_op jit(solution)/shard_map/convert_element_type | solution.py:276

commit v2 on v0

v2 whole, which is shorter than its diff:
```python
import jax
import jax.numpy as jnp
from jax import lax
from jax.experimental import pallas as pl
from jax.experimental.pallas import tpu as pltpu
from jax.sharding import PartitionSpec as P

PEERS = 16
CHIPS = 8
SECTIONS = 8
SLOTS = 16
TILE = 256
HEADS = 128
HEAD = 128
REQUESTS = 32
PHASES = 4
PHASE_HEADS = HEADS // PHASES
GROUP = 16
SCALE = HEAD ** (-0.5)
MESH = pl.DeviceIdType.MESH


def landed(ref, sem):
    pltpu.make_async_copy(ref, ref, sem).wait()


def kernel(
    q_hbm, res_hbm, k_hbm, v_hbm, len_ref, req_ref, pos_ref,
    att_ref, nxt_ref,
    q_in, res_in, q_f32, res_f32, q_send, gq0, gq1, gq2, gq3, kbuf, vbuf,
    scores, weights, sums_of, place, meta_own, twin_send, twin_x0, twin_x1, twin_x2, twin_x3, twin_meta,
    x_send, xr0, xr1, xr2, xr3, m_send, mr0, mr1, mr2, mr3, hand_send,
    q_sem, res_sem, kv_sem, gq_send_sem, gq_recv_sem, gq_twin_sem,
    twin_x_send_sem, twin_x_sem, twin_m_send_sem, twin_m_sem,
    x_send_sem, x_sem, m_send_sem, m_sem, hand_send_sem, hand_sem,
):
    gq = (gq0, gq1, gq2, gq3)
    twin_x = (twin_x0, twin_x1, twin_x2, twin_x3)
    xr = (xr0, xr1, xr2, xr3)
    mr = (mr0, mr1, mr2, mr3)
    me = lax.axis_index("peer")
    section = lax.axis_index("section")
    core, chip = lax.rem(me, 2), me // 2
    twin = me + 1 - 2 * core
    after = lax.rem(section + 1, SECTIONS)
    before = lax.rem(section + SECTIONS - 1, SECTIONS)

    barrier = pltpu.get_barrier_semaphore()

    def greet(d, carry):
        pl.semaphore_signal(
            barrier, inc=1, device_id=(section, lax.rem(me + 2 * d, PEERS)), device_id_type=MESH)
        return carry

    lax.fori_loop(1, CHIPS, greet, 0)
    pl.semaphore_signal(barrier, inc=1, device_id=(before, me), device_id_type=MESH)
    pl.semaphore_signal(barrier, inc=1, device_id=(section, twin), device_id_type=MESH)

    q_copy = pltpu.make_async_copy(q_hbm, q_in, q_sem)
    q_copy.start()
    res_copy = pltpu.make_async_copy(res_hbm, res_in, res_sem)
    res_copy.start()
    loads = []
    for p in range(PHASES):
        cols = pl.ds(p * 256, 256)
        for i, (src, dst) in enumerate(((k_hbm, kbuf), (v_hbm, vbuf))):
            load = pltpu.make_async_copy(
                src.at[0, :, :, cols], dst.at[p], kv_sem.at[p, i])
            load.start()
            loads.append(load)

    def spread(rows, out):
        for h in range(HEADS):
            piece = rows[:, h * HEAD:(h + 1) * HEAD].astype(jnp.float32)
            out[0, h:h + 1, :] = piece[0:1]
            out[1, h:h + 1, :] = piece[1:2]

    q_copy.wait()
    spread(q_in, q_f32)
    for p in range(PHASES):
        q_send[p] = q_f32[:, p * PHASE_HEADS:(p + 1) * PHASE_HEADS, :].astype(jnp.bfloat16)

    pl.semaphore_wait(barrier, CHIPS + 1)

    for p in range(PHASES):
        def send_q(d, carry, p=p):
            pltpu.make_async_remote_copy(
                src_ref=q_send.at[p], dst_ref=gq[p].at[core, chip],
                send_sem=gq_send_sem, recv_sem=gq_recv_sem.at[p],
                device_id=(section, lax.rem(me + 2 * d, PEERS)), device_id_type=MESH).start()
            return carry

        pltpu.make_async_copy(q_send.at[p], gq[p].at[core, chip], gq_recv_sem.at[p]).start()
        lax.fori_loop(1, CHIPS, send_q, 0)

    def pass_queries(p):
        landed(gq[p].at[core], gq_recv_sem.at[p])
        copy = pltpu.make_async_remote_copy(
            src_ref=gq[p].at[core], dst_ref=gq[p].at[core],
            send_sem=gq_send_sem, recv_sem=gq_twin_sem.at[p],
            device_id=(section, twin), device_id_type=MESH)
        copy.start()
        return copy

    res_copy.wait()
    spread(res_in, res_f32)

    token = lax.broadcasted_iota(jnp.int32, (PHASE_HEADS, TILE), 1)
    lane = lax.broadcasted_iota(jnp.int32, (PHASE_HEADS, 128), 1)
    zero_block = jnp.zeros((GROUP, HEAD), jnp.bfloat16)
    ones = jnp.ones((TILE, HEAD), jnp.bfloat16)
    owner = [req_ref[0, t] for t in range(SLOTS)]
    limit = [len_ref[0, owner[t]] - pos_ref[0, t] * TILE for t in range(SLOTS)]
    same = [owner[t] == owner[t - 1] for t in range(1, SLOTS)]
    last = [jnp.where(same[t], -1, owner[t]) for t in range(SLOTS - 1)] + [owner[SLOTS - 1]]
    for r in range(REQUESTS):
        at = jnp.int32(0)
        for t in range(SLOTS):
            at = jnp.where(last[t] == r, t, at)
        place[r] = at
    column = [
        jnp.where(r < 0, -128, ((r >> 1) & 1) * 64 + (r >> 2) * 4 + (r & 1)) for r in last]
    is_peak = (lane & 3) < 2

    def attend(p):
        tops = []
        for t in range(SLOTS):
            r = owner[t]
            q = gq[p][(r >> 1) & 1, r >> 2, r & 1]
            wide = jnp.concatenate(
                [jnp.concatenate([q[:GROUP], zero_block], axis=1),
                 jnp.concatenate([zero_block, q[GROUP:]], axis=1)], axis=0)
            score = lax.dot_general(
                wide, kbuf[p, t], (((1,), (1,)), ((), ())),
                preferred_element_type=jnp.float32) * SCALE
            score = jnp.where(token < limit[t], score, -jnp.inf)
            scores[t] = score
            tops.append(jnp.max(
                jnp.maximum(score[:, :128], score[:, 128:]), axis=1, keepdims=True))
        for t in range(1, SLOTS):
            tops[t] = jnp.maximum(jnp.where(same[t - 1], tops[t - 1], -jnp.inf), tops[t])
        for t in range(SLOTS - 2, -1, -1):
            tops[t] = jnp.where(same[t], tops[t + 1], tops[t])
        mix = None
        for t in range(SLOTS):
            weight = jnp.exp(scores[t] - tops[t]).astype(jnp.bfloat16)
            weights[pl.ds(PHASE_HEADS * t, PHASE_HEADS), :] = weight
            both = jnp.dot(weight, vbuf[p, t], preferred_element_type=jnp.float32)
            part = jnp.concatenate([both[:GROUP, :HEAD], both[GROUP:, HEAD:]], axis=0)
            mix = part if t == 0 else jnp.where(same[t - 1], mix, 0.0) + part
            sums_of[p, t] = mix
        sums = jnp.dot(weights[...], ones, preferred_element_type=jnp.float32)
        meta = jnp.where(is_peak, -jnp.inf, 0.0)
        total = None
        for t in range(SLOTS):
            part = sums[PHASE_HEADS * t:PHASE_HEADS * (t + 1)]
            total = part if t == 0 else jnp.where(same[t - 1], total, 0.0) + part
            meta = jnp.where(lane == column[t], tops[t], meta)
            meta = jnp.where(lane == column[t] + 2, total, meta)
        meta_own[p] = meta
        pltpu.make_async_remote_copy(
            src_ref=meta_own.at[p], dst_ref=twin_meta.at[p],
            send_sem=twin_m_send_sem, recv_sem=twin_m_sem.at[p],
            device_id=(section, twin), device_id_type=MESH).start()
        for c in range(CHIPS):
            for i in range(2):
                twin_send[p, c, i] = sums_of[p, place[4 * c + 2 * (1 - core) + i]].astype(jnp.bfloat16)
        pltpu.make_async_remote_copy(
            src_ref=twin_send.at[p], dst_ref=twin_x[p],
            send_sem=twin_x_send_sem, recv_sem=twin_x_sem.at[p],
            device_id=(section, twin), device_id_type=MESH).start()

    def join_cores(p):
        landed(meta_own.at[p], twin_m_sem.at[p])
        here = pltpu.roll(meta_own[p], 64 * core, 1)
        there = pltpu.roll(twin_meta[p], 64 * core, 1)
        peak = jnp.maximum(here, there)
        base = jnp.where(peak == -jnp.inf, 0.0, peak)
        used = is_peak & (lane < 32)
        by_here = jnp.where(used, jnp.exp(here - base), 0.0)
        by_there = jnp.where(used, jnp.exp(there - base), 0.0)
        total = by_here * pltpu.roll(here, 126, 1) + by_there * pltpu.roll(there, 126, 1)
        total = jnp.where(used, total, 0.0)
        meta = jnp.where(is_peak, peak, pltpu.roll(total, 2, 1))
        turned = jnp.concatenate(
            [meta, jnp.zeros((128 - PHASE_HEADS, 128), jnp.float32)], axis=0).T
        for c in range(CHIPS):
            m_send[p, c] = turned[4 * c:4 * c + 4]
        landed(twin_x[p], twin_x_sem.at[p])
        for c in range(CHIPS):
            for i in range(2):
                at = 4 * c + i
                own = sums_of[p, place[4 * c + 2 * core + i]]
                other = twin_x[p][c, i].astype(jnp.float32)
                x_send[p, c, i] = (
                    by_here[:, at:at + 1] * own + by_there[:, at:at + 1] * other).astype(jnp.bfloat16)

        def send_x(d, carry):
            to = lax.rem(chip + d, CHIPS)
            pltpu.make_async_remote_copy(
                src_ref=x_send.at[p, to], dst_ref=xr[p].at[chip],
                send_sem=x_send_sem, recv_sem=x_sem.at[p],
                device_id=(section, 2 * to + core), device_id_type=MESH).start()
            pltpu.make_async_remote_copy(
                src_ref=m_send.at[p, to], dst_ref=mr[p].at[chip],
                send_sem=m_send_sem, recv_sem=m_sem.at[p],
                device_id=(section, 2 * to + core), device_id_type=MESH).start()
            return carry

        lax.fori_loop(1, CHIPS, send_x, 0)
        pltpu.make_async_copy(x_send.at[p, chip], xr[p].at[chip], x_sem.at[p]).start()
        pltpu.make_async_copy(m_send.at[p, chip], mr[p].at[chip], m_sem.at[p]).start()

    def join_chips(p):
        landed(mr[p], m_sem.at[p])
        rows = jnp.concatenate([mr[p][c] for c in range(CHIPS)], axis=0)
        meta = jnp.concatenate(
            [rows, jnp.zeros((128 - 4 * CHIPS, 128), jnp.float32)], axis=0).T[:PHASE_HEADS]
        totals = pltpu.roll(meta, 126, 1)
        landed(xr[p], x_sem.at[p])
        heads = pl.ds(p * PHASE_HEADS, PHASE_HEADS)
        for i in range(2):
            used = ((lane & 3) == i) & (lane < 4 * CHIPS)
            peaks = jnp.where(used, meta, -jnp.inf)
            part = jnp.exp(peaks - jnp.max(peaks, axis=1, keepdims=True))
            whole = jnp.sum(jnp.where(used, part * totals, 0.0), axis=1, keepdims=True)
            part = part / whole
            mix = None
            for c in range(CHIPS):
                at = 4 * c + i
                term = part[:, at:at + 1] * xr[p][c, i].astype(jnp.float32)
                mix = term if mix is None else mix + term
            attended = mix.astype(jnp.bfloat16)
            att_ref[i, heads, :] = attended
            hand_send[p, i] = (
                res_f32[i, heads, :] + attended.astype(jnp.float32)).astype(jnp.bfloat16)
        pltpu.make_async_remote_copy(
            src_ref=hand_send.at[p], dst_ref=nxt_ref.at[:, heads, :],
            send_sem=hand_send_sem, recv_sem=hand_sem,
            device_id=(after, me), device_id_type=MESH).start()

    passed = [pass_queries(0), pass_queries(1)]
    for p in range(PHASES):
        passed[p].wait_recv()
        loads[2 * p].wait()
        loads[2 * p + 1].wait()
        attend(p)
        if p + 2 < PHASES:
            passed.append(pass_queries(p + 2))
        if p > 0:
            join_cores(p - 1)
    join_cores(PHASES - 1)
    for p in range(PHASES):
        join_chips(p)

    for p in range(PHASES):
        landed(gq[p].at[0, pl.ds(0, 7)], gq_send_sem)
        landed(gq[p].at[0], gq_send_sem)
        landed(x_send.at[p, pl.ds(0, 7)], x_send_sem)
        landed(m_send.at[p, pl.ds(0, 7)], m_send_sem)
    landed(twin_send, twin_x_send_sem)
    landed(meta_own, twin_m_send_sem)
    landed(hand_send, hand_send_sem)
    landed(nxt_ref, hand_sem)


def local(
    queries, residual, key_tile_store, value_tile_store, lengths, tile_request, tile_position
):
    any_spec = pl.BlockSpec(memory_space=pl.ANY)
    smem_spec = pl.BlockSpec(memory_space=pltpu.SMEM)
    vmem_spec = pl.BlockSpec(memory_space=pltpu.VMEM)
    dma = pltpu.SemaphoreType.DMA
    bf16, f32 = jnp.bfloat16, jnp.float32
    scratch = (
        [pltpu.VMEM((2, HEADS * HEAD), bf16)] * 2
        + [pltpu.VMEM((2, HEADS, HEAD), f32)] * 2
        + [pltpu.VMEM((PHASES, 2, PHASE_HEADS, HEAD), bf16)]
        + [pltpu.VMEM((2, CHIPS, 2, PHASE_HEADS, HEAD), bf16)] * PHASES
        + [pltpu.VMEM((PHASES, SLOTS, TILE, 256), bf16)] * 2
        + [pltpu.VMEM((SLOTS, PHASE_HEADS, TILE), f32), pltpu.VMEM((SLOTS * PHASE_HEADS, TILE), bf16),
           pltpu.VMEM((PHASES, SLOTS, PHASE_HEADS, HEAD), f32), pltpu.SMEM((REQUESTS,), jnp.int32),
           pltpu.VMEM((PHASES, PHASE_HEADS, 128), f32),
           pltpu.VMEM((PHASES, CHIPS, 2, PHASE_HEADS, HEAD), bf16)]
        + [pltpu.VMEM((CHIPS, 2, PHASE_HEADS, HEAD), bf16)] * PHASES
        + [pltpu.VMEM((PHASES, PHASE_HEADS, 128), f32),
           pltpu.VMEM((PHASES, CHIPS, 2, PHASE_HEADS, HEAD), bf16)]
        + [pltpu.VMEM((CHIPS, 2, PHASE_HEADS, HEAD), bf16)] * PHASES
        + [pltpu.VMEM((PHASES, CHIPS, 4, 128), f32)]
        + [pltpu.VMEM((CHIPS, 4, 128), f32)] * PHASES
        + [pltpu.VMEM((PHASES, 2, PHASE_HEADS, HEAD), bf16)]
        + [dma, dma, dma((PHASES, 2)), dma, dma((PHASES,)), dma((PHASES,)),
           dma, dma((PHASES,)), dma, dma((PHASES,)), dma, dma((PHASES,)), dma, dma((PHASES,)), dma, dma]
    )
    attended, handed = pl.pallas_call(
        kernel,
        out_shape=(jax.ShapeDtypeStruct((2, HEADS, HEAD), bf16),) * 2,
        in_specs=[any_spec] * 4 + [smem_spec] * 3,
        out_specs=[vmem_spec] * 2,
        scratch_shapes=scratch,
        compiler_params=pltpu.CompilerParams(
            collective_id=0, has_side_effects=True, vmem_limit_bytes=60 * 1024 * 1024),
    )(queries, residual, key_tile_store, value_tile_store, lengths, tile_request, tile_position)
    return attended.reshape(queries.shape), handed.reshape(queries.shape)


def solution(mesh):
    in_specs = (
        P(("section", "peer"), None),
        P(("section", "peer"), None),
        P("section", "peer", None, None),
        P("section", "peer", None, None),
        P("section", None),
        P("section", "peer"),
        P("section", "peer"),
    )
    out_specs = (P(("section", "peer"), None), P(("section", "peer"), None))
    return jax.shard_map(local, mesh=mesh, in_specs=in_specs, out_specs=out_specs, check_vma=False)
```

time: 299 us -> 38.7 us (0.13)
  waiting for transfers between devices: 140 us -> 0 us
  blocking collectives: 102 us -> 0 us
  Pallas kernels: 0 us -> 36.1 us
  local copies, waits for them, and re-layouts: 24.8 us -> 1.66 us
  between operations: 14.9 us -> 0.64 us
  matrix products: 12.3 us -> 0 us
    unnamed x3 -> x0, waiting for transfers between devices: 104 us -> none
    pmax x1 -> x0, blocking collectives: 68 us -> none  [local(): global_peak = lax.pmax(local_peak, 'peer')]
    pallas_call x0 -> x1, Pallas kernels: none -> 36.1 us  [local(): pl.pallas_call(kernel, out_shape=(jax.ShapeDtypeStruct((2, HEADS, HEAD),...]
    unnamed x1 -> x0, blocking collectives: 33.7 us -> none
    all_gather x1 -> x0, waiting for transfers between devices: 31.6 us -> none  [local(): collected_rows = lax.all_gather(queries, 'peer', axis=0, tiled=True)]
    unnamed x20 -> x0, local copies, waits for them, and re-layouts: 22.1 us -> none
    dot_general x4 -> x0, matrix products: 12.3 us -> none  [the longest x1 5.77 us: local(): jnp.einsum('tgjd,tpgd->tgjp', selected_slots, key_row_block, preferred_el...]
    ppermute x1 -> x0, waiting for transfers between devices: 4.91 us -> none  [from_behind(): return lax.ppermute(block, axis, route)]
  transfers between devices with their start and end apart: 3 -> 0, of which waited for: 3 -> 0; matrix products, arithmetic and copies ran while one was open for 7% -> 0% of each run, Pallas kernels for 0% -> 0%
where the time goes in v2:
time: 38.7 us; the launch traced here: 38.4 us
  Pallas kernels  36.1 us (93%)
  local copies, waits for them, and re-layouts  1.66 us (4%)
  between operations  0.64 us (2%)
    pallas_call x1, Pallas kernels, local(): pl.pallas_call(kernel, out_shape=(jax.ShapeDtypeStruct((2, HEADS, HEAD),...  36.1 us
    reshape x1, local copies, waits for them, and re-layouts, local(): return (attended.reshape(queries.shape), handed.reshape(queries.shape))  1.66 us

profile of v2, /device:TPU:0, one launch (start us, length us, event | category | flops | bytes accessed | tf_op | source)
XLA Modules:
  0.0 38.4 jit_solution(14285522490069646463)
XLA Ops:
  0.6 36.1 %shard_map.86 = (bf16[2,128,128]{2,1,0:T(8,128)(2,1)}, bf16[2,128,128]{2,1,0:T(8,128)(2,1)}) custom-call(bf16[2,16384]{1,0:T(2,128)(2,1)} %q_hbm.1, bf16[2,16384]{1,0:T(2,128)(2,1)} %res_hbm.1, bf16[1,16,256,1024]{3,2,1,0:T(8,128)(2,1)} %k_hbm.1, bf16[1,16,256,1024]{3,2,1,0:T(8,128)(2,1)} %v_hbm.1, s32[1,32]{1,0:T(1,128)} %len_ref.1, s32[1,16]{1,0:T(1,128)} %req_ref.1, ...), custom_call_target="tpu_custom_call" | custom-call | tf_op jit(solution)/shard_map/pallas_call | solution.py:295
  36.7 1.7 %copy_bitcast_fusion = (bf16[2,16384]{1,0:T(2,128)(2,1)}, bf16[2,16384]{1,0:T(2,128)(2,1)}) fusion(bf16[1,2,128,128]{3,2,1,0:T(8,128)(2,1)} %bitcast.7, bf16[1,2,128,128]{3,2,1,0:T(8,128)(2,1)} %bitcast.6), kind=kLoop, calls=%fused_computation | loop fusion | bytes 262144 | tf_op jit(solution)/shard_map/reshape | solution.py:304

commit v3 on v2

v3 whole, which is shorter than its diff:
```python
import jax
import jax.numpy as jnp
from jax import lax
from jax.experimental import pallas as pl
from jax.experimental.pallas import tpu as pltpu
from jax.sharding import PartitionSpec as P

PEERS = 16
CHIPS = 8
SECTIONS = 8
SLOTS = 16
TILE = 256
HEADS = 128
HEAD = 128
REQUESTS = 32
GROUP = 16
WIDTHS = (2, 2, 2, 2)
PHASES = len(WIDTHS)
FIRST = [sum(WIDTHS[:p]) for p in range(PHASES)]
ROWS = [GROUP * w for w in WIDTHS]
SCALE = HEAD ** (-0.5)
NONE = -1e30
STEPS = ((1, 2), (1, 1), (1, 3), (1, 0), (0, 2), (0, 1), (0, 3))
WIDE = [-(-4 * r // 128) for r in ROWS]
BLOCKS = [2 * r + 16 for r in ROWS]
MESH = pl.DeviceIdType.MESH


def widen(block):
    rest = 128 - block.shape[1]
    if not rest:
        return block
    return jnp.concatenate([block, jnp.zeros((block.shape[0], rest), block.dtype)], axis=1)


def landed(ref, sem):
    pltpu.make_async_copy(ref, ref, sem).wait()


def kernel(
    q_hbm, res_hbm, k_hbm, v_hbm, len_hbm, req_hbm, pos_hbm,
    att_ref, nxt_ref,
    len_ref, req_ref, pos_ref, q_in, res_in, q_f32, res_f32, place, *rest,
):
    q_send, gq, kbuf, vbuf, scores, sums_of, meta_own, twin_meta, twin_send, twin_x, x_send, xr, hand_send = (
        rest[i * PHASES:(i + 1) * PHASES] for i in range(13))
    (
        q_sem, res_sem, plan_sem, kv_sem, gq_send_sem, gq_recv_sem, gq_twin_sem,
        twin_x_send_sem, twin_x_sem, twin_m_send_sem, twin_m_sem,
        x_send_sem, x_sem, hand_send_sem, hand_sem,
    ) = rest[13 * PHASES:]
    me = lax.axis_index("peer")
    section = lax.axis_index("section")
    core, chip = lax.rem(me, 2), me // 2
    y, z = chip // 4, lax.rem(chip, 4)
    others = [lax.rem(y + dy, 2) * 4 + lax.rem(z + dz, 4) for dy, dz in STEPS]
    twin = me + 1 - 2 * core
    after = lax.rem(section + 1, SECTIONS)
    before = lax.rem(section + SECTIONS - 1, SECTIONS)

    barrier = pltpu.get_barrier_semaphore()

    for to in others:
        pl.semaphore_signal(
            barrier, inc=1, device_id=(section, 2 * to + core), device_id_type=MESH)
    pl.semaphore_signal(barrier, inc=1, device_id=(before, me), device_id_type=MESH)
    pl.semaphore_signal(barrier, inc=1, device_id=(section, twin), device_id_type=MESH)

    q_copy = pltpu.make_async_copy(q_hbm, q_in, q_sem)
    q_copy.start()
    res_copy = pltpu.make_async_copy(res_hbm, res_in, res_sem)
    res_copy.start()
    plan = []
    for i, (src, dst) in enumerate(((len_hbm, len_ref), (req_hbm, req_ref), (pos_hbm, pos_ref))):
        plan.append(pltpu.make_async_copy(src, dst, plan_sem.at[i]))
        plan[i].start()
    def spread(rows, out):
        for h in range(HEADS):
            piece = rows[:, h * HEAD:(h + 1) * HEAD].astype(jnp.float32)
            out[0, h:h + 1, :] = piece[0:1]
            out[1, h:h + 1, :] = piece[1:2]

    q_copy.wait()
    spread(q_in, q_f32)
    for p in range(PHASES):
        q_send[p][...] = q_f32[:, GROUP * FIRST[p]:GROUP * FIRST[p] + ROWS[p], :].astype(jnp.bfloat16)

    pl.semaphore_wait(barrier, CHIPS + 1)

    for p in range(PHASES):
        for to in others:
            pltpu.make_async_remote_copy(
                src_ref=q_send[p], dst_ref=gq[p].at[core, chip],
                send_sem=gq_send_sem.at[p], recv_sem=gq_recv_sem.at[p],
                device_id=(section, 2 * to + core), device_id_type=MESH).start()
        pltpu.make_async_copy(q_send[p], gq[p].at[core, chip], gq_recv_sem.at[p]).start()
    loads = []
    for p in range(PHASES):
        cols = pl.ds(FIRST[p] * HEAD, WIDTHS[p] * HEAD)
        for i, (src, dst) in enumerate(((k_hbm, kbuf), (v_hbm, vbuf))):
            load = pltpu.make_async_copy(
                src.at[0, :, :, cols], dst[p], kv_sem.at[p, i])
            load.start()
            loads.append(load)

    def pass_queries(p):
        landed(gq[p].at[core], gq_recv_sem.at[p])
        copy = pltpu.make_async_remote_copy(
            src_ref=gq[p].at[core], dst_ref=gq[p].at[core],
            send_sem=gq_send_sem.at[p], recv_sem=gq_twin_sem.at[p],
            device_id=(section, twin), device_id_type=MESH)
        copy.start()
        return copy

    res_copy.wait()
    spread(res_in, res_f32)
    for copy in plan:
        copy.wait()

    token = lax.broadcasted_iota(jnp.int32, (1, TILE), 1)
    owner = [req_ref[0, t] for t in range(SLOTS)]
    limit = [len_ref[0, owner[t]] - pos_ref[0, t] * TILE for t in range(SLOTS)]
    same = [owner[t] == owner[t - 1] for t in range(1, SLOTS)]
    last = [jnp.where(same[t], -1, owner[t]) for t in range(SLOTS - 1)] + [owner[SLOTS - 1]]
    for r in range(REQUESTS):
        at = jnp.int32(0)
        for t in range(SLOTS):
            at = jnp.where(last[t] == r, t, at)
        place[r] = at
    column = [
        jnp.where(r < 0, -128, ((r >> 1) & 1) * 64 + (r & 1) * 8 + (r >> 2)) for r in last]

    def lanes(p):
        return lax.broadcasted_iota(jnp.int32, (ROWS[p], 128), 1)

    def attend(p):
        lane = lanes(p)
        tops = []
        for t in range(SLOTS):
            r = owner[t]
            q = gq[p][(r >> 1) & 1, r >> 2, r & 1]
            score = jnp.concatenate(
                [lax.dot_general(
                    q[GROUP * g:GROUP * (g + 1)], kbuf[p][t, :, HEAD * g:HEAD * (g + 1)],
                    (((1,), (1,)), ((), ())), preferred_element_type=jnp.float32)
                 for g in range(WIDTHS[p])], axis=0) * SCALE
            score = jnp.where(token < limit[t], score, -jnp.inf)
            scores[p][t] = score
            tops.append(jnp.max(
                jnp.maximum(score[:, :128], score[:, 128:]), axis=1, keepdims=True))
        for t in range(1, SLOTS):
            tops[t] = jnp.maximum(jnp.where(same[t - 1], tops[t - 1], -jnp.inf), tops[t])
        for t in range(SLOTS - 2, -1, -1):
            tops[t] = jnp.where(same[t], tops[t + 1], tops[t])
        mix, total = None, None
        meta = jnp.where((lane & 63) < 16, NONE, 0.0)
        for t in range(SLOTS):
            weight = jnp.exp(scores[p][t] - tops[t]).astype(jnp.bfloat16)
            part = jnp.concatenate(
                [jnp.dot(
                    weight[GROUP * g:GROUP * (g + 1)], vbuf[p][t, :, HEAD * g:HEAD * (g + 1)],
                    preferred_element_type=jnp.float32)
                 for g in range(WIDTHS[p])], axis=0)
            wide = weight.astype(jnp.float32)
            count = jnp.sum(wide[:, :128] + wide[:, 128:], axis=1, keepdims=True)
            mix = part if t == 0 else jnp.where(same[t - 1], mix, 0.0) + part
            total = count if t == 0 else jnp.where(same[t - 1], total, 0.0) + count
            sums_of[p][t] = mix
            meta = jnp.where(lane == column[t], tops[t], meta)
            meta = jnp.where(lane == column[t] + 16, total, meta)
        meta_own[p][...] = meta
        pltpu.make_async_remote_copy(
            src_ref=meta_own[p], dst_ref=twin_meta[p],
            send_sem=twin_m_send_sem.at[p], recv_sem=twin_m_sem.at[p],
            device_id=(section, twin), device_id_type=MESH).start()
        for c in range(CHIPS):
            for i in range(2):
                twin_send[p][c, i] = sums_of[p][place[4 * c + 2 * (1 - core) + i]].astype(jnp.bfloat16)
        pltpu.make_async_remote_copy(
            src_ref=twin_send[p], dst_ref=twin_x[p],
            send_sem=twin_x_send_sem.at[p], recv_sem=twin_x_sem.at[p],
            device_id=(section, twin), device_id_type=MESH).start()

    def join_cores(p):
        lane, rows = lanes(p), ROWS[p]
        landed(twin_meta[p], twin_m_sem.at[p])
        here = pltpu.roll(meta_own[p][...], 64 * core, 1)
        there = pltpu.roll(twin_meta[p][...], 64 * core, 1)
        peak = jnp.maximum(here, there)
        by_here, by_there = jnp.exp(here - peak), jnp.exp(there - peak)
        total = by_here * pltpu.roll(here, 112, 1) + by_there * pltpu.roll(there, 112, 1)
        meta = jnp.where(lane < 16, peak, jnp.where(lane < 32, pltpu.roll(total, 16, 1), 0.0))
        turned = jnp.concatenate([meta, jnp.zeros((128 - rows, 128), jnp.float32)], axis=0).T
        kinds = [turned[CHIPS * i:CHIPS * (i + 1), :rows] for i in range(4)]
        per = 4 // WIDE[p]
        lines = [
            widen(jnp.concatenate(kinds[per * j:per * (j + 1)], axis=1)) for j in range(WIDE[p])]
        split = []
        for line in lines:
            high = line.astype(jnp.bfloat16).astype(jnp.float32)
            middle = (line - high).astype(jnp.bfloat16).astype(jnp.float32)
            split += [high, middle, line - high - middle]
        for c in range(CHIPS):
            x_send[p][c, 2 * rows:, :] = jnp.concatenate(
                [part[c:c + 1] for part in split]
                + [jnp.zeros((16 - len(split), 128), jnp.float32)], axis=0).astype(jnp.bfloat16)
        landed(twin_x[p], twin_x_sem.at[p])
        for c in range(CHIPS):
            for i in range(2):
                at = 8 * i + c
                own = sums_of[p][place[4 * c + 2 * core + i]]
                other = twin_x[p][c, i].astype(jnp.float32)
                x_send[p][c, rows * i:rows * (i + 1), :] = (
                    by_here[:, at:at + 1] * own + by_there[:, at:at + 1] * other).astype(jnp.bfloat16)
        for to in others:
            pltpu.make_async_remote_copy(
                src_ref=x_send[p].at[to], dst_ref=xr[p].at[chip],
                send_sem=x_send_sem.at[p], recv_sem=x_sem.at[p],
                device_id=(section, 2 * to + core), device_id_type=MESH).start()
        pltpu.make_async_copy(x_send[p].at[chip], xr[p].at[chip], x_sem.at[p]).start()

    def join_chips(p):
        lane, rows, got = lanes(p), ROWS[p], xr[p]
        landed(got, x_sem.at[p])
        heads = pl.ds(GROUP * FIRST[p], rows)
        per = 4 // WIDE[p]
        lines = [[] for _ in range(WIDE[p])]
        for c in range(CHIPS):
            tile = got[c, 2 * rows:, :].astype(jnp.float32)
            for j in range(WIDE[p]):
                lines[j].append(tile[3 * j:3 * j + 1] + tile[3 * j + 1:3 * j + 2] + tile[3 * j + 2:3 * j + 3])
        lines = [jnp.concatenate(line, axis=0) for line in lines]
        kinds = jnp.concatenate(
            [lines[i // per][:, rows * (i % per):rows * (i % per + 1)] for i in range(4)], axis=0)
        meta = jnp.concatenate([widen(kinds), jnp.zeros((128 - 32, 128), jnp.float32)], axis=0).T[:rows]
        totals = pltpu.roll(meta, 112, 1)
        for i in range(2):
            used = (lane >> 3) == i
            peaks = jnp.where(used, meta, NONE)
            part = jnp.exp(peaks - jnp.max(peaks, axis=1, keepdims=True))
            whole = jnp.sum(jnp.where(used, part * totals, 0.0), axis=1, keepdims=True)
            part = part / whole
            mix = None
            for c in range(CHIPS):
                at = 8 * i + c
                term = part[:, at:at + 1] * got[c, rows * i:rows * (i + 1), :].astype(jnp.float32)
                mix = term if mix is None else mix + term
            attended = mix.astype(jnp.bfloat16)
            att_ref[i, heads, :] = attended
            hand_send[p][i] = (
                res_f32[i, heads, :] + attended.astype(jnp.float32)).astype(jnp.bfloat16)
        pltpu.make_async_remote_copy(
            src_ref=hand_send[p], dst_ref=nxt_ref.at[:, heads, :],
            send_sem=hand_send_sem.at[p], recv_sem=hand_sem,
            device_id=(after, me), device_id_type=MESH).start()

    passed = [pass_queries(0), pass_queries(1)]
    for p in range(PHASES):
        passed[p].wait_recv()
        loads[2 * p].wait()
        loads[2 * p + 1].wait()
        attend(p)
        if p + 2 < PHASES:
            passed.append(pass_queries(p + 2))
        if p > 0:
            join_cores(p - 1)
    join_cores(PHASES - 1)
    for p in range(PHASES):
        join_chips(p)

    for p in range(PHASES):
        landed(gq[p].at[0, pl.ds(0, 7)], gq_send_sem.at[p])
        landed(gq[p].at[0], gq_send_sem.at[p])
        landed(x_send[p].at[pl.ds(0, 7)], x_send_sem.at[p])
        landed(twin_send[p], twin_x_send_sem.at[p])
        landed(meta_own[p], twin_m_send_sem.at[p])
        landed(hand_send[p], hand_send_sem.at[p])
    landed(nxt_ref, hand_sem)


def local(
    queries, residual, key_tile_store, value_tile_store, lengths, tile_request, tile_position
):
    any_spec = pl.BlockSpec(memory_space=pl.ANY)
    vmem_spec = pl.BlockSpec(memory_space=pltpu.VMEM)
    dma = pltpu.SemaphoreType.DMA
    bf16, f32 = jnp.bfloat16, jnp.float32
    def each(dtype, shape):
        return [pltpu.VMEM(shape(w, r, n), dtype) for w, r, n in zip(WIDTHS, ROWS, BLOCKS, strict=True)]

    sums = (CHIPS, 2)
    scratch = (
        [pltpu.SMEM(a.shape, jnp.int32) for a in (lengths, tile_request, tile_position)]
        + [pltpu.VMEM((2, HEADS * HEAD), bf16)] * 2
        + [pltpu.VMEM((2, HEADS, HEAD), f32)] * 2
        + [pltpu.SMEM((REQUESTS,), jnp.int32)]
        + each(bf16, lambda w, r, n: (2, r, HEAD))
        + each(bf16, lambda w, r, n: (2, *sums, r, HEAD))
        + each(bf16, lambda w, r, n: (SLOTS, TILE, w * HEAD)) * 2
        + each(f32, lambda w, r, n: (SLOTS, r, TILE))
        + each(f32, lambda w, r, n: (SLOTS, r, HEAD))
        + each(f32, lambda w, r, n: (r, 128)) * 2
        + each(bf16, lambda w, r, n: (*sums, r, HEAD)) * 2
        + each(bf16, lambda w, r, n: (CHIPS, n, HEAD)) * 2
        + each(bf16, lambda w, r, n: (2, r, HEAD))
        + [dma, dma, dma((3,)), dma((PHASES, 2))] + [dma((PHASES,))] * 10 + [dma]
    )
    attended, handed = pl.pallas_call(
        kernel,
        out_shape=(pltpu.VMEM((2, HEADS, HEAD), bf16),) * 2,
        in_specs=[any_spec] * 7,
        out_specs=[vmem_spec] * 2,
        scratch_shapes=scratch,
        compiler_params=pltpu.CompilerParams(
            collective_id=0, has_side_effects=True, vmem_limit_bytes=60 * 1024 * 1024),
    )(queries, residual, key_tile_store, value_tile_store, lengths, tile_request, tile_position)
    return attended.reshape(queries.shape), handed.reshape(queries.shape)


def solution(mesh):
    in_specs = (
        P(("section", "peer"), None),
        P(("section", "peer"), None),
        P("section", "peer", None, None),
        P("section", "peer", None, None),
        P("section", None),
        P("section", "peer"),
        P("section", "peer"),
    )
    out_specs = (P(("section", "peer"), None), P(("section", "peer"), None))
    return jax.shard_map(local, mesh=mesh, in_specs=in_specs, out_specs=out_specs, check_vma=False)
```

time: 38.7 us -> 34.4 us (0.89)
  Pallas kernels: 36.1 us -> 32.8 us
  local copies, waits for them, and re-layouts: 1.66 us -> 0.79 us
    pallas_call x1, Pallas kernels: 36.1 us -> 32.8 us  [local(): pl.pallas_call(kernel, out_shape=(pltpu.VMEM((2, HEADS, HEAD), bf16),) *...]
    reshape x1, local copies, waits for them, and re-layouts: 1.66 us -> 0.79 us  [local(): return (attended.reshape(queries.shape), handed.reshape(queries.shape))]
where the time goes in v3:
time: 34.4 us; the launch traced here: 34.2 us
  Pallas kernels  32.8 us (95%)
  local copies, waits for them, and re-layouts  0.79 us (2%)
  between operations  0.64 us (2%)
    pallas_call x1, Pallas kernels, local(): pl.pallas_call(kernel, out_shape=(pltpu.VMEM((2, HEADS, HEAD), bf16),) *...  32.8 us
    reshape x1, local copies, waits for them, and re-layouts, local(): return (attended.reshape(queries.shape), handed.reshape(queries.shape))  0.79 us

profile of v3, /device:TPU:0, one launch (start us, length us, event | category | flops | bytes accessed | tf_op | source)
XLA Modules:
  0.0 34.2 jit_solution(7461773416320992131)
XLA Ops:
  0.6 32.8 %shard_map.86 = (bf16[2,128,128]{2,1,0:T(8,128)(2,1)S(1)}, bf16[2,128,128]{2,1,0:T(8,128)(2,1)S(1)}) custom-call(bf16[2,16384]{1,0:T(2,128)(2,1)} %q_hbm.1, bf16[2,16384]{1,0:T(2,128)(2,1)} %res_hbm.1, bf16[1,16,256,1024]{3,2,1,0:T(8,128)(2,1)} %k_hbm.1, bf16[1,16,256,1024]{3,2,1,0:T(8,128)(2,1)} %v_hbm.1, s32[1,32]{1,0:T(1,128)} %len_hbm.1, ...), custom_call_target="tpu_custom_call" | custom-call | tf_op jit(solution)/shard_map/pallas_call | solution.py:308
  33.4 0.8 %copy_bitcast_fusion = (bf16[2,16384]{1,0:T(2,128)(2,1)}, bf16[2,16384]{1,0:T(2,128)(2,1)}) fusion(bf16[1,2,128,128]{3,2,1,0:T(8,128)(2,1)S(1)} %bitcast.7, bf16[1,2,128,128]{3,2,1,0:T(8,128)(2,1)S(1)} %bitcast.6), kind=kLoop, calls=%fused_computation | loop fusion | bytes 262144 | tf_op jit(solution)/shard_map/reshape | solution.py:317

commit v4 on v3

--- a/solution.py
+++ b/solution.py
@@ -16,21 +16,13 @@
 GROUP = 16
 WIDTHS = (2, 2, 2, 2)
 PHASES = len(WIDTHS)
+LAST = PHASES - 1
 FIRST = [sum(WIDTHS[:p]) for p in range(PHASES)]
 ROWS = [GROUP * w for w in WIDTHS]
 SCALE = HEAD ** (-0.5)
 NONE = -1e30
 STEPS = ((1, 2), (1, 1), (1, 3), (1, 0), (0, 2), (0, 1), (0, 3))
-WIDE = [-(-4 * r // 128) for r in ROWS]
-BLOCKS = [2 * r + 16 for r in ROWS]
 MESH = pl.DeviceIdType.MESH
-
-
-def widen(block):
-    rest = 128 - block.shape[1]
-    if not rest:
-        return block
-    return jnp.concatenate([block, jnp.zeros((block.shape[0], rest), block.dtype)], axis=1)
 
 
 def landed(ref, sem):
@@ -40,15 +32,16 @@
 def kernel(
     q_hbm, res_hbm, k_hbm, v_hbm, len_hbm, req_hbm, pos_hbm,
     att_ref, nxt_ref,
-    len_ref, req_ref, pos_ref, q_in, res_in, q_f32, res_f32, place, *rest,
+    len_ref, req_ref, pos_ref, q_in, res_in, q_f32, res_f32, res_send, prev_res, y_got, ym_got, place, *rest,
 ):
-    q_send, gq, kbuf, vbuf, scores, sums_of, meta_own, twin_meta, twin_send, twin_x, x_send, xr, hand_send = (
-        rest[i * PHASES:(i + 1) * PHASES] for i in range(13))
+    q_send, gq, kbuf, vbuf, scores, sums_of, meta_own, twin_meta, twin_send, twin_x, x_send, xr, m_send, mr, hand_send = (
+        rest[i * PHASES:(i + 1) * PHASES] for i in range(15))
     (
         q_sem, res_sem, plan_sem, kv_sem, gq_send_sem, gq_recv_sem, gq_twin_sem,
         twin_x_send_sem, twin_x_sem, twin_m_send_sem, twin_m_sem,
-        x_send_sem, x_sem, hand_send_sem, hand_sem,
-    ) = rest[13 * PHASES:]
+        x_send_sem, x_sem, m_send_sem, m_sem, hand_send_sem, hand_sem,
+        res_send_sem, prev_res_sem, y_send_sem, y_sem, ym_send_sem, ym_sem,
+    ) = rest[15 * PHASES:]
     me = lax.axis_index("peer")
     section = lax.axis_index("section")
     core, chip = lax.rem(me, 2), me // 2
@@ -114,6 +107,11 @@
 
     res_copy.wait()
     spread(res_in, res_f32)
+    res_send[...] = res_f32[:, GROUP * FIRST[LAST]:, :].astype(jnp.bfloat16)
+    pass_residual = pltpu.make_async_remote_copy(
+        src_ref=res_send, dst_ref=prev_res, send_sem=res_send_sem, recv_sem=prev_res_sem,
+        device_id=(after, me), device_id_type=MESH)
+    pass_residual.start()
     for copy in plan:
         copy.wait()
 
@@ -191,49 +189,48 @@
         total = by_here * pltpu.roll(here, 112, 1) + by_there * pltpu.roll(there, 112, 1)
         meta = jnp.where(lane < 16, peak, jnp.where(lane < 32, pltpu.roll(total, 16, 1), 0.0))
         turned = jnp.concatenate([meta, jnp.zeros((128 - rows, 128), jnp.float32)], axis=0).T
-        kinds = [turned[CHIPS * i:CHIPS * (i + 1), :rows] for i in range(4)]
-        per = 4 // WIDE[p]
-        lines = [
-            widen(jnp.concatenate(kinds[per * j:per * (j + 1)], axis=1)) for j in range(WIDE[p])]
-        split = []
-        for line in lines:
-            high = line.astype(jnp.bfloat16).astype(jnp.float32)
-            middle = (line - high).astype(jnp.bfloat16).astype(jnp.float32)
-            split += [high, middle, line - high - middle]
+        table = jnp.concatenate([turned[CHIPS * i:CHIPS * (i + 1), :rows] for i in range(4)], axis=1)
         for c in range(CHIPS):
-            x_send[p][c, 2 * rows:, :] = jnp.concatenate(
-                [part[c:c + 1] for part in split]
-                + [jnp.zeros((16 - len(split), 128), jnp.float32)], axis=0).astype(jnp.bfloat16)
+            m_send[p][c] = table[c:c + 1]
         landed(twin_x[p], twin_x_sem.at[p])
         for c in range(CHIPS):
             for i in range(2):
                 at = 8 * i + c
                 own = sums_of[p][place[4 * c + 2 * core + i]]
                 other = twin_x[p][c, i].astype(jnp.float32)
-                x_send[p][c, rows * i:rows * (i + 1), :] = (
+                x_send[p][c, i] = (
                     by_here[:, at:at + 1] * own + by_there[:, at:at + 1] * other).astype(jnp.bfloat16)
+        if p == LAST:
+            for to in others + [chip]:
+                pltpu.make_async_remote_copy(
+                    src_ref=x_send[p].at[to], dst_ref=y_got.at[chip],
+                    send_sem=y_send_sem, recv_sem=y_sem,
+                    device_id=(after, 2 * to + core), device_id_type=MESH).start()
+                pltpu.make_async_remote_copy(
+                    src_ref=m_send[p].at[to], dst_ref=ym_got.at[chip],
+                    send_sem=ym_send_sem, recv_sem=ym_sem,
+                    device_id=(after, 2 * to + core), device_id_type=MESH).start()
         for to in others:
             pltpu.make_async_remote_copy(
                 src_ref=x_send[p].at[to], dst_ref=xr[p].at[chip],
                 send_sem=x_send_sem.at[p], recv_sem=x_sem.at[p],
                 device_id=(section, 2 * to + core), device_id_type=MESH).start()
+            pltpu.make_async_remote_copy(
+                src_ref=m_send[p].at[to], dst_ref=mr[p].at[chip],
+                send_sem=m_send_sem.at[p], recv_sem=m_sem.at[p],
+                device_id=(section, 2 * to + core), device_id_type=MESH).start()
         pltpu.make_async_copy(x_send[p].at[chip], xr[p].at[chip], x_sem.at[p]).start()
-
-    def join_chips(p):
-        lane, rows, got = lanes(p), ROWS[p], xr[p]
-        landed(got, x_sem.at[p])
-        heads = pl.ds(GROUP * FIRST[p], rows)
-        per = 4 // WIDE[p]
-        lines = [[] for _ in range(WIDE[p])]
-        for c in range(CHIPS):
-            tile = got[c, 2 * rows:, :].astype(jnp.float32)
-            for j in range(WIDE[p]):
-                lines[j].append(tile[3 * j:3 * j + 1] + tile[3 * j + 1:3 * j + 2] + tile[3 * j + 2:3 * j + 3])
-        lines = [jnp.concatenate(line, axis=0) for line in lines]
-        kinds = jnp.concatenate(
-            [lines[i // per][:, rows * (i % per):rows * (i % per + 1)] for i in range(4)], axis=0)
-        meta = jnp.concatenate([widen(kinds), jnp.zeros((128 - 32, 128), jnp.float32)], axis=0).T[:rows]
+        pltpu.make_async_copy(m_send[p].at[chip], mr[p].at[chip], m_sem.at[p]).start()
+
+    def join_chips(p, got, got_sem, lines, lines_sem, finish):
+        lane, rows = lanes(p), ROWS[p]
+        landed(lines, lines_sem)
+        table = jnp.concatenate([lines[c] for c in range(CHIPS)], axis=0)
+        kinds = jnp.concatenate([table[:, rows * i:rows * (i + 1)] for i in range(4)], axis=0)
+        kinds = jnp.concatenate([kinds, jnp.zeros((32, 128 - rows), jnp.float32)], axis=1)
+        meta = jnp.concatenate([kinds, jnp.zeros((128 - 32, 128), jnp.float32)], axis=0).T[:rows]
         totals = pltpu.roll(meta, 112, 1)
+        landed(got, got_sem)
         for i in range(2):
             used = (lane >> 3) == i
             peaks = jnp.where(used, meta, NONE)
@@ -243,16 +240,32 @@
             mix = None
             for c in range(CHIPS):
                 at = 8 * i + c
-                term = part[:, at:at + 1] * got[c, rows * i:rows * (i + 1), :].astype(jnp.float32)
+                term = part[:, at:at + 1] * got[c, i].astype(jnp.float32)
                 mix = term if mix is None else mix + term
-            attended = mix.astype(jnp.bfloat16)
+            finish(i, mix.astype(jnp.bfloat16))
+
+    def finish_here(p):
+        heads = pl.ds(GROUP * FIRST[p], ROWS[p])
+
+        def finish(i, attended):
             att_ref[i, heads, :] = attended
-            hand_send[p][i] = (
-                res_f32[i, heads, :] + attended.astype(jnp.float32)).astype(jnp.bfloat16)
-        pltpu.make_async_remote_copy(
-            src_ref=hand_send[p], dst_ref=nxt_ref.at[:, heads, :],
-            send_sem=hand_send_sem.at[p], recv_sem=hand_sem,
-            device_id=(after, me), device_id_type=MESH).start()
+            if p < LAST:
+                hand_send[p][i] = (
+                    res_f32[i, heads, :] + attended.astype(jnp.float32)).astype(jnp.bfloat16)
+
+        join_chips(p, xr[p], x_sem.at[p], mr[p], m_sem.at[p], finish)
+        if p < LAST:
+            pltpu.make_async_remote_copy(
+                src_ref=hand_send[p], dst_ref=nxt_ref.at[:, heads, :],
+                send_sem=hand_send_sem.at[p], recv_sem=hand_sem,
+                device_id=(after, me), device_id_type=MESH).start()
+
+    def finish_before():
+        def finish(i, attended):
+            nxt_ref[i, GROUP * FIRST[LAST]:, :] = (
+                prev_res[i].astype(jnp.float32) + attended.astype(jnp.float32)).astype(jnp.bfloat16)
+
+        join_chips(LAST, y_got, y_sem, ym_got, ym_sem, finish)
 
     passed = [pass_queries(0), pass_queries(1)]
     for p in range(PHASES):
@@ -266,16 +279,22 @@
             join_cores(p - 1)
     join_cores(PHASES - 1)
     for p in range(PHASES):
-        join_chips(p)
+        finish_here(p)
+    pass_residual.wait()
+    finish_before()
 
     for p in range(PHASES):
         landed(gq[p].at[0, pl.ds(0, 7)], gq_send_sem.at[p])
         landed(gq[p].at[0], gq_send_sem.at[p])
         landed(x_send[p].at[pl.ds(0, 7)], x_send_sem.at[p])
+        landed(m_send[p].at[pl.ds(0, 7)], m_send_sem.at[p])
         landed(twin_send[p], twin_x_send_sem.at[p])
         landed(meta_own[p], twin_m_send_sem.at[p])
-        landed(hand_send[p], hand_send_sem.at[p])
-    landed(nxt_ref, hand_sem)
+        if p < LAST:
+            landed(hand_send[p], hand_send_sem.at[p])
+    landed(x_send[LAST], y_send_sem)
+    landed(m_send[LAST], ym_send_sem)
+    landed(nxt_ref.at[:, pl.ds(0, GROUP * FIRST[LAST]), :], hand_sem)
 
 
 def local(
@@ -286,24 +305,27 @@
     dma = pltpu.SemaphoreType.DMA
     bf16, f32 = jnp.bfloat16, jnp.float32
     def each(dtype, shape):
-        return [pltpu.VMEM(shape(w, r, n), dtype) for w, r, n in zip(WIDTHS, ROWS, BLOCKS, strict=True)]
+        return [pltpu.VMEM(shape(w, r), dtype) for w, r in zip(WIDTHS, ROWS, strict=True)]
 
     sums = (CHIPS, 2)
     scratch = (
         [pltpu.SMEM(a.shape, jnp.int32) for a in (lengths, tile_request, tile_position)]
         + [pltpu.VMEM((2, HEADS * HEAD), bf16)] * 2
         + [pltpu.VMEM((2, HEADS, HEAD), f32)] * 2
+        + [pltpu.VMEM((2, ROWS[LAST], HEAD), bf16)] * 2
+        + [pltpu.VMEM((CHIPS, 2, ROWS[LAST], HEAD), bf16), pltpu.VMEM((CHIPS, 1, 4 * ROWS[LAST]), f32)]
         + [pltpu.SMEM((REQUESTS,), jnp.int32)]
-        + each(bf16, lambda w, r, n: (2, r, HEAD))
-        + each(bf16, lambda w, r, n: (2, *sums, r, HEAD))
-        + each(bf16, lambda w, r, n: (SLOTS, TILE, w * HEAD)) * 2
-        + each(f32, lambda w, r, n: (SLOTS, r, TILE))
-        + each(f32, lambda w, r, n: (SLOTS, r, HEAD))
-        + each(f32, lambda w, r, n: (r, 128)) * 2
-        + each(bf16, lambda w, r, n: (*sums, r, HEAD)) * 2
-        + each(bf16, lambda w, r, n: (CHIPS, n, HEAD)) * 2
-        + each(bf16, lambda w, r, n: (2, r, HEAD))
-        + [dma, dma, dma((3,)), dma((PHASES, 2))] + [dma((PHASES,))] * 10 + [dma]
+        + each(bf16, lambda w, r: (2, r, HEAD))
+        + each(bf16, lambda w, r: (2, *sums, r, HEAD))
+        + each(bf16, lambda w, r: (SLOTS, TILE, w * HEAD)) * 2
+        + each(f32, lambda w, r: (SLOTS, r, TILE))
+        + each(f32, lambda w, r: (SLOTS, r, HEAD))
+        + each(f32, lambda w, r: (r, 128)) * 2
+        + each(bf16, lambda w, r: (*sums, r, HEAD)) * 2
+        + each(bf16, lambda w, r: (*sums, r, HEAD)) * 2
+        + each(f32, lambda w, r: (CHIPS, 1, 4 * r)) * 2
+        + each(bf16, lambda w, r: (2, r, HEAD))
+        + [dma, dma, dma((3,)), dma((PHASES, 2))] + [dma((PHASES,))] * 12 + [dma] * 7
     )
     attended, handed = pl.pallas_call(
         kernel,

time: 34.4 us -> 33 us (0.959)
  Pallas kernels: 32.8 us -> 31.4 us
    pallas_call x1, Pallas kernels: 32.8 us -> 31.4 us  [local(): pl.pallas_call(kernel, out_shape=(pltpu.VMEM((2, HEADS, HEAD), bf16),) *...]
where the time goes in v4:
time: 33 us; the launch traced here: 32.8 us
  Pallas kernels  31.4 us (95%)
  local copies, waits for them, and re-layouts  0.79 us (2%)
  between operations  0.64 us (2%)
    pallas_call x1, Pallas kernels, local(): pl.pallas_call(kernel, out_shape=(pltpu.VMEM((2, HEADS, HEAD), bf16),) *...  31.4 us
    reshape x1, local copies, waits for them, and re-layouts, local(): return (attended.reshape(queries.shape), handed.reshape(queries.shape))  0.79 us

profile of v4, /device:TPU:0, one launch (start us, length us, event | category | flops | bytes accessed | tf_op | source)
XLA Modules:
  0.0 32.8 jit_solution(189235554589377240)
XLA Ops:
  0.6 31.4 %shard_map.86 = (bf16[2,128,128]{2,1,0:T(8,128)(2,1)S(1)}, bf16[2,128,128]{2,1,0:T(8,128)(2,1)S(1)}) custom-call(bf16[2,16384]{1,0:T(2,128)(2,1)} %q_hbm.1, bf16[2,16384]{1,0:T(2,128)(2,1)} %res_hbm.1, bf16[1,16,256,1024]{3,2,1,0:T(8,128)(2,1)} %k_hbm.1, bf16[1,16,256,1024]{3,2,1,0:T(8,128)(2,1)} %v_hbm.1, s32[1,32]{1,0:T(1,128)} %len_hbm.1, ...), custom_call_target="tpu_custom_call" | custom-call | tf_op jit(solution)/shard_map/pallas_call | solution.py:330
  32.1 0.8 %copy_bitcast_fusion = (bf16[2,16384]{1,0:T(2,128)(2,1)}, bf16[2,16384]{1,0:T(2,128)(2,1)}) fusion(bf16[1,2,128,128]{3,2,1,0:T(8,128)(2,1)S(1)} %bitcast.7, bf16[1,2,128,128]{3,2,1,0:T(8,128)(2,1)S(1)} %bitcast.6), kind=kLoop, calls=%fused_computation | loop fusion | bytes 262144 | tf_op jit(solution)/shard_map/reshape | solution.py:339

commit v5 on v4

--- a/solution.py
+++ b/solution.py
@@ -16,6 +16,8 @@
 GROUP = 16
 WIDTHS = (2, 2, 2, 2)
 PHASES = len(WIDTHS)
+TWICE = 3
+EARLY = 1
 LAST = PHASES - 1
 FIRST = [sum(WIDTHS[:p]) for p in range(PHASES)]
 ROWS = [GROUP * w for w in WIDTHS]
@@ -25,6 +27,13 @@
 MESH = pl.DeviceIdType.MESH
 
 
+def widen(block):
+    rest = 128 - block.shape[1]
+    if not rest:
+        return block
+    return jnp.concatenate([block, jnp.zeros((block.shape[0], rest), block.dtype)], axis=1)
+
+
 def landed(ref, sem):
     pltpu.make_async_copy(ref, ref, sem).wait()
 
@@ -32,7 +41,7 @@
 def kernel(
     q_hbm, res_hbm, k_hbm, v_hbm, len_hbm, req_hbm, pos_hbm,
     att_ref, nxt_ref,
-    len_ref, req_ref, pos_ref, q_in, res_in, q_f32, res_f32, res_send, prev_res, y_got, ym_got, place, *rest,
+    len_ref, req_ref, pos_ref, q_in, res_in, q_f32, res_f32, res_send, prev_res, place, *rest,
 ):
     q_send, gq, kbuf, vbuf, scores, sums_of, meta_own, twin_meta, twin_send, twin_x, x_send, xr, m_send, mr, hand_send = (
         rest[i * PHASES:(i + 1) * PHASES] for i in range(15))
@@ -41,7 +50,9 @@
         twin_x_send_sem, twin_x_sem, twin_m_send_sem, twin_m_sem,
         x_send_sem, x_sem, m_send_sem, m_sem, hand_send_sem, hand_sem,
         res_send_sem, prev_res_sem, y_send_sem, y_sem, ym_send_sem, ym_sem,
-    ) = rest[15 * PHASES:]
+    ) = rest[15 * PHASES + 2 * (PHASES - TWICE):]
+    y_got = rest[15 * PHASES:][:PHASES - TWICE]
+    ym_got = rest[15 * PHASES:][PHASES - TWICE:2 * (PHASES - TWICE)]
     me = lax.axis_index("peer")
     section = lax.axis_index("section")
     core, chip = lax.rem(me, 2), me // 2
@@ -107,7 +118,7 @@
 
     res_copy.wait()
     spread(res_in, res_f32)
-    res_send[...] = res_f32[:, GROUP * FIRST[LAST]:, :].astype(jnp.bfloat16)
+    res_send[...] = res_f32[:, GROUP * FIRST[TWICE]:, :].astype(jnp.bfloat16)
     pass_residual = pltpu.make_async_remote_copy(
         src_ref=res_send, dst_ref=prev_res, send_sem=res_send_sem, recv_sem=prev_res_sem,
         device_id=(after, me), device_id_type=MESH)
@@ -189,7 +200,8 @@
         total = by_here * pltpu.roll(here, 112, 1) + by_there * pltpu.roll(there, 112, 1)
         meta = jnp.where(lane < 16, peak, jnp.where(lane < 32, pltpu.roll(total, 16, 1), 0.0))
         turned = jnp.concatenate([meta, jnp.zeros((128 - rows, 128), jnp.float32)], axis=0).T
-        table = jnp.concatenate([turned[CHIPS * i:CHIPS * (i + 1), :rows] for i in range(4)], axis=1)
+        table = widen(jnp.concatenate(
+            [turned[CHIPS * i:CHIPS * (i + 1), :rows] for i in range(4)], axis=1))
         for c in range(CHIPS):
             m_send[p][c] = table[c:c + 1]
         landed(twin_x[p], twin_x_sem.at[p])
@@ -200,15 +212,15 @@
                 other = twin_x[p][c, i].astype(jnp.float32)
                 x_send[p][c, i] = (
                     by_here[:, at:at + 1] * own + by_there[:, at:at + 1] * other).astype(jnp.bfloat16)
-        if p == LAST:
+        if p >= TWICE:
             for to in others + [chip]:
                 pltpu.make_async_remote_copy(
-                    src_ref=x_send[p].at[to], dst_ref=y_got.at[chip],
-                    send_sem=y_send_sem, recv_sem=y_sem,
+                    src_ref=x_send[p].at[to], dst_ref=y_got[p - TWICE].at[chip],
+                    send_sem=y_send_sem.at[p - TWICE], recv_sem=y_sem.at[p - TWICE],
                     device_id=(after, 2 * to + core), device_id_type=MESH).start()
                 pltpu.make_async_remote_copy(
-                    src_ref=m_send[p].at[to], dst_ref=ym_got.at[chip],
-                    send_sem=ym_send_sem, recv_sem=ym_sem,
+                    src_ref=m_send[p].at[to], dst_ref=ym_got[p - TWICE].at[chip],
+                    send_sem=ym_send_sem.at[p - TWICE], recv_sem=ym_sem.at[p - TWICE],
                     device_id=(after, 2 * to + core), device_id_type=MESH).start()
         for to in others:
             pltpu.make_async_remote_copy(
@@ -249,23 +261,27 @@
 
         def finish(i, attended):
             att_ref[i, heads, :] = attended
-            if p < LAST:
+            if p < TWICE:
                 hand_send[p][i] = (
                     res_f32[i, heads, :] + attended.astype(jnp.float32)).astype(jnp.bfloat16)
 
         join_chips(p, xr[p], x_sem.at[p], mr[p], m_sem.at[p], finish)
-        if p < LAST:
+        if p < TWICE:
             pltpu.make_async_remote_copy(
                 src_ref=hand_send[p], dst_ref=nxt_ref.at[:, heads, :],
                 send_sem=hand_send_sem.at[p], recv_sem=hand_sem,
                 device_id=(after, me), device_id_type=MESH).start()
 
-    def finish_before():
+    def finish_before(p):
+        heads = pl.ds(GROUP * FIRST[p], ROWS[p])
+        rows = pl.ds(GROUP * (FIRST[p] - FIRST[TWICE]), ROWS[p])
+        k = p - TWICE
+
         def finish(i, attended):
-            nxt_ref[i, GROUP * FIRST[LAST]:, :] = (
-                prev_res[i].astype(jnp.float32) + attended.astype(jnp.float32)).astype(jnp.bfloat16)
-
-        join_chips(LAST, y_got, y_sem, ym_got, ym_sem, finish)
+            nxt_ref[i, heads, :] = (
+                prev_res[i, rows, :].astype(jnp.float32) + attended.astype(jnp.float32)).astype(jnp.bfloat16)
+
+        join_chips(p, y_got[k], y_sem.at[k], ym_got[k], ym_sem.at[k], finish)
 
     passed = [pass_queries(0), pass_queries(1)]
     for p in range(PHASES):
@@ -277,11 +293,15 @@
             passed.append(pass_queries(p + 2))
         if p > 0:
             join_cores(p - 1)
-    join_cores(PHASES - 1)
-    for p in range(PHASES):
+    for p in range(EARLY):
         finish_here(p)
-    pass_residual.wait()
-    finish_before()
+    join_cores(LAST)
+    for p in range(EARLY, PHASES):
+        finish_here(p)
+        if p == TWICE - 1:
+            pass_residual.wait()
+        if p >= TWICE:
+            finish_before(p)
 
     for p in range(PHASES):
         landed(gq[p].at[0, pl.ds(0, 7)], gq_send_sem.at[p])
@@ -290,11 +310,12 @@
         landed(m_send[p].at[pl.ds(0, 7)], m_send_sem.at[p])
         landed(twin_send[p], twin_x_send_sem.at[p])
         landed(meta_own[p], twin_m_send_sem.at[p])
-        if p < LAST:
+        if p < TWICE:
             landed(hand_send[p], hand_send_sem.at[p])
-    landed(x_send[LAST], y_send_sem)
-    landed(m_send[LAST], ym_send_sem)
-    landed(nxt_ref.at[:, pl.ds(0, GROUP * FIRST[LAST]), :], hand_sem)
+    for p in range(TWICE, PHASES):
+        landed(x_send[p], y_send_sem.at[p - TWICE])
+        landed(m_send[p], ym_send_sem.at[p - TWICE])
+    landed(nxt_ref.at[:, pl.ds(0, GROUP * FIRST[TWICE]), :], hand_sem)
 
 
 def local(
@@ -312,8 +333,7 @@
         [pltpu.SMEM(a.shape, jnp.int32) for a in (lengths, tile_request, tile_position)]
         + [pltpu.VMEM((2, HEADS * HEAD), bf16)] * 2
         + [pltpu.VMEM((2, HEADS, HEAD), f32)] * 2
-        + [pltpu.VMEM((2, ROWS[LAST], HEAD), bf16)] * 2
-        + [pltpu.VMEM((CHIPS, 2, ROWS[LAST], HEAD), bf16), pltpu.VMEM((CHIPS, 1, 4 * ROWS[LAST]), f32)]
+        + [pltpu.VMEM((2, HEADS - GROUP * FIRST[TWICE], HEAD), bf16)] * 2
         + [pltpu.SMEM((REQUESTS,), jnp.int32)]
         + each(bf16, lambda w, r: (2, r, HEAD))
         + each(bf16, lambda w, r: (2, *sums, r, HEAD))
@@ -323,9 +343,11 @@
         + each(f32, lambda w, r: (r, 128)) * 2
         + each(bf16, lambda w, r: (*sums, r, HEAD)) * 2
         + each(bf16, lambda w, r: (*sums, r, HEAD)) * 2
-        + each(f32, lambda w, r: (CHIPS, 1, 4 * r)) * 2
+        + each(f32, lambda w, r: (CHIPS, 1, 128)) * 2
         + each(bf16, lambda w, r: (2, r, HEAD))
-        + [dma, dma, dma((3,)), dma((PHASES, 2))] + [dma((PHASES,))] * 12 + [dma] * 7
+        + each(bf16, lambda w, r: (*sums, r, HEAD))[TWICE:]
+        + each(f32, lambda w, r: (CHIPS, 1, 128))[TWICE:]
+        + [dma, dma, dma((3,)), dma((PHASES, 2))] + [dma((PHASES,))] * 12 + [dma] * 3 + [dma((PHASES - TWICE,))] * 4
     )
     attended, handed = pl.pallas_call(
         kernel,

time: 33 us -> 32.7 us (level)
  no operation moved by 1% of the time
where the time goes in v5:
time: 32.7 us; the launch traced here: 32.5 us
  Pallas kernels  31.1 us (95%)
  local copies, waits for them, and re-layouts  0.79 us (2%)
  between operations  0.64 us (2%)
    pallas_call x1, Pallas kernels, local(): pl.pallas_call(kernel, out_shape=(pltpu.VMEM((2, HEADS, HEAD), bf16),) *...  31.1 us
    reshape x1, local copies, waits for them, and re-layouts, local(): return (attended.reshape(queries.shape), handed.reshape(queries.shape))  0.79 us

profile of v5, /device:TPU:0, one launch (start us, length us, event | category | flops | bytes accessed | tf_op | source)
XLA Modules:
  0.0 32.5 jit_solution(16254467193772708644)
XLA Ops:
  0.6 31.1 %shard_map.86 = (bf16[2,128,128]{2,1,0:T(8,128)(2,1)S(1)}, bf16[2,128,128]{2,1,0:T(8,128)(2,1)S(1)}) custom-call(bf16[2,16384]{1,0:T(2,128)(2,1)} %q_hbm.1, bf16[2,16384]{1,0:T(2,128)(2,1)} %res_hbm.1, bf16[1,16,256,1024]{3,2,1,0:T(8,128)(2,1)} %k_hbm.1, bf16[1,16,256,1024]{3,2,1,0:T(8,128)(2,1)} %v_hbm.1, s32[1,32]{1,0:T(1,128)} %len_hbm.1, ...), custom_call_target="tpu_custom_call" | custom-call | tf_op jit(solution)/shard_map/pallas_call | solution.py:352
  31.7 0.8 %copy_bitcast_fusion = (bf16[2,16384]{1,0:T(2,128)(2,1)}, bf16[2,16384]{1,0:T(2,128)(2,1)}) fusion(bf16[1,2,128,128]{3,2,1,0:T(8,128)(2,1)S(1)} %bitcast.7, bf16[1,2,128,128]{3,2,1,0:T(8,128)(2,1)S(1)} %bitcast.6), kind=kLoop, calls=%fused_computation | loop fusion | bytes 262144 | tf_op jit(solution)/shard_map/reshape | solution.py:361

commit v6 on v5

--- a/solution.py
+++ b/solution.py
@@ -204,6 +204,18 @@
             [turned[CHIPS * i:CHIPS * (i + 1), :rows] for i in range(4)], axis=1))
         for c in range(CHIPS):
             m_send[p][c] = table[c:c + 1]
+        if p >= TWICE:
+            for to in others + [chip]:
+                pltpu.make_async_remote_copy(
+                    src_ref=m_send[p].at[to], dst_ref=ym_got[p - TWICE].at[chip],
+                    send_sem=ym_send_sem.at[p - TWICE], recv_sem=ym_sem.at[p - TWICE],
+                    device_id=(after, 2 * to + core), device_id_type=MESH).start()
+        for to in others:
+            pltpu.make_async_remote_copy(
+                src_ref=m_send[p].at[to], dst_ref=mr[p].at[chip],
+                send_sem=m_send_sem.at[p], recv_sem=m_sem.at[p],
+                device_id=(section, 2 * to + core), device_id_type=MESH).start()
+        pltpu.make_async_copy(m_send[p].at[chip], mr[p].at[chip], m_sem.at[p]).start()
         landed(twin_x[p], twin_x_sem.at[p])
         for c in range(CHIPS):
             for i in range(2):
@@ -218,21 +230,12 @@
                     src_ref=x_send[p].at[to], dst_ref=y_got[p - TWICE].at[chip],
                     send_sem=y_send_sem.at[p - TWICE], recv_sem=y_sem.at[p - TWICE],
                     device_id=(after, 2 * to + core), device_id_type=MESH).start()
-                pltpu.make_async_remote_copy(
-                    src_ref=m_send[p].at[to], dst_ref=ym_got[p - TWICE].at[chip],
-                    send_sem=ym_send_sem.at[p - TWICE], recv_sem=ym_sem.at[p - TWICE],
-                    device_id=(after, 2 * to + core), device_id_type=MESH).start()
         for to in others:
             pltpu.make_async_remote_copy(
                 src_ref=x_send[p].at[to], dst_ref=xr[p].at[chip],
                 send_sem=x_send_sem.at[p], recv_sem=x_sem.at[p],
                 device_id=(section, 2 * to + core), device_id_type=MESH).start()
-            pltpu.make_async_remote_copy(
-                src_ref=m_send[p].at[to], dst_ref=mr[p].at[chip],
-                send_sem=m_send_sem.at[p], recv_sem=m_sem.at[p],
-                device_id=(section, 2 * to + core), device_id_type=MESH).start()
         pltpu.make_async_copy(x_send[p].at[chip], xr[p].at[chip], x_sem.at[p]).start()
-        pltpu.make_async_copy(m_send[p].at[chip], mr[p].at[chip], m_sem.at[p]).start()
 
     def join_chips(p, got, got_sem, lines, lines_sem, finish):
         lane, rows = lanes(p), ROWS[p]

time: 32.7 us -> 32.3 us (0.988)
  Pallas kernels: 31.1 us -> 30.7 us
    pallas_call x1, Pallas kernels: 31.1 us -> 30.7 us  [local(): pl.pallas_call(kernel, out_shape=(pltpu.VMEM((2, HEADS, HEAD), bf16),) *...]
where the time goes in v6:
time: 32.3 us; the launch traced here: 32.2 us
  Pallas kernels  30.7 us (95%)
  local copies, waits for them, and re-layouts  0.79 us (2%)
  between operations  0.64 us (2%)
    pallas_call x1, Pallas kernels, local(): pl.pallas_call(kernel, out_shape=(pltpu.VMEM((2, HEADS, HEAD), bf16),) *...  30.7 us
    reshape x1, local copies, waits for them, and re-layouts, local(): return (attended.reshape(queries.shape), handed.reshape(queries.shape))  0.79 us

profile of v6, /device:TPU:0, one launch (start us, length us, event | category | flops | bytes accessed | tf_op | source)
XLA Modules:
  0.0 32.2 jit_solution(5541396697610884442)
XLA Ops:
  0.6 30.7 %shard_map.86 = (bf16[2,128,128]{2,1,0:T(8,128)(2,1)S(1)}, bf16[2,128,128]{2,1,0:T(8,128)(2,1)S(1)}) custom-call(bf16[2,16384]{1,0:T(2,128)(2,1)} %q_hbm.1, bf16[2,16384]{1,0:T(2,128)(2,1)} %res_hbm.1, bf16[1,16,256,1024]{3,2,1,0:T(8,128)(2,1)} %k_hbm.1, bf16[1,16,256,1024]{3,2,1,0:T(8,128)(2,1)} %v_hbm.1, s32[1,32]{1,0:T(1,128)} %len_hbm.1, ...), custom_call_target="tpu_custom_call" | custom-call | tf_op jit(solution)/shard_map/pallas_call | solution.py:355
  31.4 0.8 %copy_bitcast_fusion = (bf16[2,16384]{1,0:T(2,128)(2,1)}, bf16[2,16384]{1,0:T(2,128)(2,1)}) fusion(bf16[1,2,128,128]{3,2,1,0:T(8,128)(2,1)S(1)} %bitcast.7, bf16[1,2,128,128]{3,2,1,0:T(8,128)(2,1)S(1)} %bitcast.6), kind=kLoop, calls=%fused_computation | loop fusion | bytes 262144 | tf_op jit(solution)/shard_map/reshape | solution.py:364

commit v7 on v6

--- a/solution.py
+++ b/solution.py
@@ -190,7 +190,7 @@
             send_sem=twin_x_send_sem.at[p], recv_sem=twin_x_sem.at[p],
             device_id=(section, twin), device_id_type=MESH).start()
 
-    def join_cores(p):
+    def join_cores(p, meanwhile=()):
         lane, rows = lanes(p), ROWS[p]
         landed(twin_meta[p], twin_m_sem.at[p])
         here = pltpu.roll(meta_own[p][...], 64 * core, 1)
@@ -216,6 +216,8 @@
                 send_sem=m_send_sem.at[p], recv_sem=m_sem.at[p],
                 device_id=(section, 2 * to + core), device_id_type=MESH).start()
         pltpu.make_async_copy(m_send[p].at[chip], mr[p].at[chip], m_sem.at[p]).start()
+        for earlier in meanwhile:
+            finish_here(earlier)
         landed(twin_x[p], twin_x_sem.at[p])
         for c in range(CHIPS):
             for i in range(2):
@@ -296,9 +298,7 @@
             passed.append(pass_queries(p + 2))
         if p > 0:
             join_cores(p - 1)
-    for p in range(EARLY):
-        finish_here(p)
-    join_cores(LAST)
+    join_cores(LAST, range(EARLY))
     for p in range(EARLY, PHASES):
         finish_here(p)
         if p == TWICE - 1:

time: 32.3 us -> 32.5 us (level)
  no operation moved by 1% of the time
where the time goes in v7:
time: 32.5 us; the launch traced here: 32.3 us
  Pallas kernels  30.9 us (95%)
  local copies, waits for them, and re-layouts  0.79 us (2%)
  between operations  0.64 us (2%)
    pallas_call x1, Pallas kernels, local(): pl.pallas_call(kernel, out_shape=(pltpu.VMEM((2, HEADS, HEAD), bf16),) *...  30.9 us
    reshape x1, local copies, waits for them, and re-layouts, local(): return (attended.reshape(queries.shape), handed.reshape(queries.shape))  0.79 us

profile of v7, /device:TPU:0, one launch (start us, length us, event | category | flops | bytes accessed | tf_op | source)
XLA Modules:
  0.0 32.3 jit_solution(961355049901308986)
XLA Ops:
  0.6 30.9 %shard_map.86 = (bf16[2,128,128]{2,1,0:T(8,128)(2,1)S(1)}, bf16[2,128,128]{2,1,0:T(8,128)(2,1)S(1)}) custom-call(bf16[2,16384]{1,0:T(2,128)(2,1)} %q_hbm.1, bf16[2,16384]{1,0:T(2,128)(2,1)} %res_hbm.1, bf16[1,16,256,1024]{3,2,1,0:T(8,128)(2,1)} %k_hbm.1, bf16[1,16,256,1024]{3,2,1,0:T(8,128)(2,1)} %v_hbm.1, s32[1,32]{1,0:T(1,128)} %len_hbm.1, ...), custom_call_target="tpu_custom_call" | custom-call | tf_op jit(solution)/shard_map/pallas_call | solution.py:355
  31.5 0.8 %copy_bitcast_fusion = (bf16[2,16384]{1,0:T(2,128)(2,1)}, bf16[2,16384]{1,0:T(2,128)(2,1)}) fusion(bf16[1,2,128,128]{3,2,1,0:T(8,128)(2,1)S(1)} %bitcast.7, bf16[1,2,128,128]{3,2,1,0:T(8,128)(2,1)S(1)} %bitcast.6), kind=kLoop, calls=%fused_computation | loop fusion | bytes 262144 | tf_op jit(solution)/shard_map/reshape | solution.py:364
